TPU v7x, 32 devices: a whole 2x2x4 slice. The times are simulated.
32 devices in a mesh: dp: 8 (over y, x, core), tensor: 4 (over z).
Axes of the slice: x: 2, y: 2, z: 4, core: 2. Of those that a mesh axis runs over, the one named last changes fastest.
Arguments:
- block_input: bfloat16 [512, 50, 512], P(('dp', 'tensor')), may hold values from -6 to 6
- position_kernel: bfloat16 [3, 3, 512], replicated, may hold values from -2 to 2
- position_bias: bfloat16 [512], replicated, may hold values from -1.75 to 1.75
- early_gain: bfloat16 [512], replicated, may hold values from 0.5 to 1.5
- early_shift: bfloat16 [512], replicated, may hold values from -1.25 to 1.25
- joint_weight: bfloat16 [512, 1536], replicated, may hold values from -0.375 to 0.375
- joint_bias: bfloat16 [1024], replicated, may hold values from -1.75 to 1.75
- small_kernel: bfloat16 [3, 3, 128], replicated, may hold values from -2 to 2
- small_bias: bfloat16 [128], replicated, may hold values from -1.75 to 1.75
- middle_kernel: bfloat16 [5, 5, 192], replicated, may hold values from -1.25 to 1.25
- middle_bias: bfloat16 [192], replicated, may hold values from -1.75 to 1.75
- large_kernel: bfloat16 [7, 7, 192], replicated, may hold values from -0.875 to 0.875
- large_bias: bfloat16 [192], replicated, may hold values from -1.75 to 1.75
- output_weight: bfloat16 [512, 512], P('tensor'), may hold values from -0.25 to 0.25
- output_bias: bfloat16 [512], replicated, may hold values from -1.25 to 1.25
- late_gain: bfloat16 [512], replicated, may hold values from 0.5 to 1.5
- late_shift: bfloat16 [512], replicated, may hold values from -1.25 to 1.25
- expand_weight: bfloat16 [512, 2048], P(None, 'tensor'), may hold values from -0.25 to 0.25
- expand_bias: bfloat16 [2048], P('tensor'), may hold values from -1.75 to 1.75
- reduce_weight: bfloat16 [2048, 512], P('tensor'), may hold values from -0.125 to 0.125
- reduce_bias: bfloat16 [512], replicated, may hold values from -1.25 to 1.25
- cotangent: bfloat16 [512, 50, 512], P(('dp', 'tensor')), may hold values from -6 to 6
Outputs:
- block_output: bfloat16 [512, 50, 512], P(('dp', 'tensor'))
- input_grad: bfloat16 [512, 50, 512], P(('dp', 'tensor'))
- grad_position_kernel: float32 [3, 3, 512], replicated
- grad_position_bias: float32 [512], replicated
- grad_early_gain: float32 [512], replicated
- grad_early_shift: float32 [512], replicated
- grad_joint_weight: float32 [512, 1536], replicated
- grad_joint_bias: float32 [1024], replicated
- grad_small_kernel: float32 [3, 3, 128], replicated
- grad_small_bias: float32 [128], replicated
- grad_middle_kernel: float32 [5, 5, 192], replicated
- grad_middle_bias: float32 [192], replicated
- grad_large_kernel: float32 [7, 7, 192], replicated
- grad_large_bias: float32 [192], replicated
- grad_output_weight: float32 [512, 512], P('tensor')
- grad_output_bias: float32 [512], replicated
- grad_late_gain: float32 [512], replicated
- grad_late_shift: float32 [512], replicated
- grad_expand_weight: float32 [512, 2048], P(None, 'tensor')
- grad_expand_bias: float32 [2048], P('tensor')
- grad_reduce_weight: float32 [2048, 512], P('tensor')
- grad_reduce_bias: float32 [512], replicated
All inputs are finite; a program needn't handle non-finite values.
Results may differ from a plain program's by a relative error of at most 0.019.
Values may be sent and summed in bfloat16 or wider, within the bound.
A program may use at most 256 MiB of HBM per device.

v0:
```python
from functools import partial

import jax
import jax.numpy as jnp
from jax import lax
from jax.sharding import PartitionSpec as P

HEADS = 8
HEAD = 64
GRID = 7


norm_eps = 1e-06


def layer_norm(values_in, norm_gain, norm_shift):
    centre = jnp.mean(values_in, axis=-1, keepdims=True)
    centred = values_in - centre
    spread = jnp.mean(centred * centred, axis=-1, keepdims=True)
    return centred * lax.rsqrt(spread + norm_eps) * norm_gain + norm_shift


def depthwise(field, kernel):
    extent = kernel.shape[0]
    margin = extent // 2
    side_len = field.shape[1]
    padded = jnp.pad(field, ((0, 0), (margin, margin), (margin, margin), (0, 0)))
    result = jnp.zeros_like(field)
    for row_tap in range(extent):
        for col_tap in range(extent):
            result = (
                result
                + padded[:, row_tap : row_tap + side_len, col_tap : col_tap + side_len, :]
                * kernel[row_tap, col_tap]
            )
    return result


def full_kernel(small_kernel, middle_kernel, large_kernel):
    small_pad = jnp.pad(small_kernel, ((2, 2), (2, 2), (0, 0)))
    middle_pad = jnp.pad(middle_kernel, ((1, 1), (1, 1), (0, 0)))
    return jnp.concatenate([small_pad, middle_pad, large_kernel], axis=2)


def position_mix(field, kernel, bias_vec):
    return field + depthwise(field, kernel) + bias_vec


def per_device(
    block_input,
    position_kernel,
    position_bias,
    early_gain,
    early_shift,
    joint_weight,
    joint_bias,
    small_kernel,
    small_bias,
    middle_kernel,
    middle_bias,
    large_kernel,
    large_bias,
    output_weight,
    output_bias,
    late_gain,
    late_shift,
    expand_weight,
    expand_bias,
    reduce_weight,
    reduce_bias,
    cotangent,
):
    f32 = jnp.float32
    bf16 = jnp.bfloat16
    image_count, token_count, model_width = block_input.shape
    row_count = image_count * token_count
    part_count = lax.axis_size("tensor")
    head_width = model_width // part_count
    heads_here = HEADS // part_count
    first_chan = lax.axis_index("tensor") * head_width
    head_scale = HEAD ** (-0.5)
    grid_cells = GRID * GRID
    inputs_f = block_input.astype(f32)
    grid_in = inputs_f[:, 1:].reshape(image_count, GRID, GRID, model_width)
    mixed_grid, pull_position = jax.vjp(
        position_mix, grid_in, position_kernel.astype(f32), position_bias.astype(f32)
    )
    first_sum = jnp.concatenate(
        [inputs_f[:, :1], mixed_grid.reshape(image_count, grid_cells, model_width)], axis=1
    )
    first_sum = first_sum.reshape(row_count, model_width)
    normed_f, pull_early = jax.vjp(
        layer_norm, first_sum, early_gain.astype(f32), early_shift.astype(f32)
    )
    normed_one = normed_f.astype(bf16)
    projected = jnp.dot(normed_one, joint_weight, preferred_element_type=f32)
    joint_f = joint_bias.astype(f32)
    img_shape = (image_count, token_count, model_width)
    query_img = (projected[:, :model_width] + joint_f[:model_width]).astype(bf16).reshape(img_shape)
    key_img = projected[:, model_width : 2 * model_width].astype(bf16).reshape(img_shape)
    value_img = (
        (projected[:, 2 * model_width :] + joint_f[model_width:]).astype(bf16).reshape(img_shape)
    )
    query_loc, key_loc, value_loc = (
        lax.all_to_all(query_img, "tensor", split_axis=2, concat_axis=0, tiled=True),
        lax.all_to_all(key_img, "tensor", split_axis=2, concat_axis=0, tiled=True),
        lax.all_to_all(value_img, "tensor", split_axis=2, concat_axis=0, tiled=True),
    )
    group_size = query_loc.shape[0]
    head_shape = (group_size, token_count, heads_here, HEAD)
    query_split = query_loc.reshape(head_shape)
    key_split = key_loc.reshape(head_shape)
    value_split = value_loc.reshape(head_shape)
    key_soft = jax.nn.softmax(key_split.astype(f32), axis=1)
    key_soft_low = key_soft.astype(bf16)
    context = jnp.einsum(
        "bnhk,bnhv->bhkv", key_soft_low, value_split, preferred_element_type=f32
    ).astype(bf16)
    factor = (
        jnp.einsum("bnhk,bhkv->bnhv", query_split, context, preferred_element_type=f32) * head_scale
    )

    def relative_term(
        query_grid, value_grid, small_w, small_b, middle_w, middle_b, large_w, large_b
    ):
        kernel_mine = lax.dynamic_slice_in_dim(
            full_kernel(small_w, middle_w, large_w), first_chan, head_width, 2
        )
        bias_mine = lax.dynamic_slice_in_dim(
            jnp.concatenate([small_b, middle_b, large_b]), first_chan, head_width, 0
        )
        conv_grid = depthwise(value_grid, kernel_mine) + bias_mine
        return query_grid * conv_grid.reshape(query_grid.shape)

    query_grid = query_loc[:, 1:].astype(f32)
    value_grid = value_loc[:, 1:].astype(f32).reshape(group_size, GRID, GRID, head_width)
    relative, pull_relative = jax.vjp(
        relative_term,
        query_grid,
        value_grid,
        small_kernel.astype(f32),
        small_bias.astype(f32),
        middle_kernel.astype(f32),
        middle_bias.astype(f32),
        large_kernel.astype(f32),
        large_bias.astype(f32),
    )
    zero_row = jnp.zeros((group_size, 1, head_width), f32)
    attention = (
        factor.reshape(group_size, token_count, head_width)
        + jnp.concatenate([zero_row, relative], axis=1)
    ).astype(bf16)
    attention_flat = attention.reshape(group_size * token_count, head_width)
    branch_out = lax.psum_scatter(
        jnp.dot(attention_flat, output_weight, preferred_element_type=f32).astype(jnp.bfloat16),
        "tensor",
        scatter_dimension=0,
        tiled=True,
    ).astype(jnp.float32)
    second_sum = first_sum + branch_out + output_bias.astype(f32)
    normed_two_f, pull_late = jax.vjp(
        layer_norm, second_sum, late_gain.astype(f32), late_shift.astype(f32)
    )
    normed_two = normed_two_f.astype(bf16)
    exact_gelu = partial(jax.nn.gelu, approximate=False)
    grad_flat = cotangent.reshape(row_count, model_width)
    normed_group = lax.all_gather(normed_two, "tensor", axis=0, tiled=True)
    pre_gelu = jnp.dot(
        normed_group, expand_weight, preferred_element_type=f32
    ) + expand_bias.astype(f32)
    activated, pull_gelu = jax.vjp(exact_gelu, pre_gelu)
    hidden_low = activated.astype(bf16)
    feed_out = lax.psum_scatter(
        jnp.dot(
            lax.slice_in_dim(hidden_low, 0, lax.axis_size("tensor") * row_count, axis=0),
            reduce_weight,
            preferred_element_type=f32,
        ).astype(jnp.bfloat16),
        "tensor",
        scatter_dimension=0,
        tiled=True,
    ).astype(jnp.float32)
    block_output = (second_sum + feed_out + reduce_bias.astype(f32)).astype(bf16).reshape(img_shape)
    grad_out_f = grad_flat.astype(f32)
    grad_reduce_bias = jnp.sum(grad_out_f, axis=0)
    grad_group = lax.all_gather(grad_flat, "tensor", axis=0, tiled=True)
    grad_reduce_weight = jnp.dot(hidden_low.T, grad_group, preferred_element_type=f32)
    grad_hidden = jnp.dot(grad_group, reduce_weight.T, preferred_element_type=f32)
    grad_pre = pull_gelu(grad_hidden)[0].astype(bf16)
    grad_expand_bias = jnp.sum(grad_pre.astype(f32), axis=0)
    grad_expand_weight = jnp.dot(normed_group.T, grad_pre, preferred_element_type=f32)
    grad_normed_two = lax.psum_scatter(
        jnp.dot(grad_pre, expand_weight.T, preferred_element_type=f32).astype(jnp.bfloat16),
        "tensor",
        scatter_dimension=0,
        tiled=True,
    ).astype(jnp.float32)
    grad_second_norm, grad_late_gain, grad_late_shift = pull_late(grad_normed_two)
    grad_second = grad_out_f + grad_second_norm
    grad_branch = grad_second.astype(bf16)
    grad_output_bias = jnp.sum(grad_branch.astype(f32), axis=0)
    branch_group = lax.all_gather(grad_branch, "tensor", axis=0, tiled=True)
    grad_output_weight = jnp.dot(attention_flat.T, branch_group, preferred_element_type=f32)
    grad_attention = jnp.dot(branch_group, output_weight.T, preferred_element_type=f32).astype(bf16)
    grad_attention = grad_attention.reshape(group_size, token_count, head_width)
    grad_att_split = grad_attention.reshape(head_shape)
    grad_query_ctx = (
        jnp.einsum("bnhv,bhkv->bnhk", grad_att_split, context, preferred_element_type=f32)
        * head_scale
    )
    grad_context = (
        jnp.einsum("bnhk,bnhv->bhkv", query_split, grad_att_split, preferred_element_type=f32)
        * head_scale
    ).astype(bf16)
    grad_key_soft = jnp.einsum(
        "bnhv,bhkv->bnhk", value_split, grad_context, preferred_element_type=f32
    )
    grad_value_ctx = jnp.einsum(
        "bnhk,bhkv->bnhv", key_soft_low, grad_context, preferred_element_type=f32
    )
    grad_key_split = key_soft * (
        grad_key_soft - jnp.sum(grad_key_soft * key_soft, axis=1, keepdims=True)
    )
    (
        grad_query_grid,
        grad_value_grid,
        grad_small_kernel,
        grad_small_bias,
        grad_middle_kernel,
        grad_middle_bias,
        grad_large_kernel,
        grad_large_bias,
    ) = pull_relative(grad_attention[:, 1:].astype(f32))
    loc_shape = (group_size, token_count, head_width)
    grad_query_loc = (
        grad_query_ctx.reshape(loc_shape) + jnp.concatenate([zero_row, grad_query_grid], axis=1)
    ).astype(bf16)
    grad_key_loc = grad_key_split.reshape(loc_shape).astype(bf16)
    grad_value_loc = (
        grad_value_ctx.reshape(loc_shape)
        + jnp.concatenate(
            [zero_row, grad_value_grid.reshape(group_size, grid_cells, head_width)], axis=1
        )
    ).astype(bf16)
    grad_query_img, grad_key_img, grad_value_img = (
        lax.all_to_all(grad_query_loc, "tensor", split_axis=0, concat_axis=2, tiled=True),
        lax.all_to_all(grad_key_loc, "tensor", split_axis=0, concat_axis=2, tiled=True),
        lax.all_to_all(grad_value_loc, "tensor", split_axis=0, concat_axis=2, tiled=True),
    )
    grad_projected = jnp.concatenate(
        [grad_query_img, grad_key_img, grad_value_img], axis=2
    ).reshape(row_count, 3 * model_width)
    grad_joint_weight = jnp.dot(normed_one.T, grad_projected, preferred_element_type=f32)
    grad_joint_bias = jnp.concatenate(
        [
            jnp.sum(grad_query_img.astype(f32), axis=(0, 1)),
            jnp.sum(grad_value_img.astype(f32), axis=(0, 1)),
        ]
    )
    grad_normed_one = jnp.dot(grad_projected, joint_weight.T, preferred_element_type=f32)
    grad_first_norm, grad_early_gain, grad_early_shift = pull_early(grad_normed_one)
    grad_first = (grad_second + grad_first_norm).reshape(img_shape)
    grad_grid, grad_position_kernel, grad_position_bias = pull_position(
        grad_first[:, 1:].reshape(image_count, GRID, GRID, model_width)
    )
    input_grad = jnp.concatenate(
        [grad_first[:, :1], grad_grid.reshape(image_count, grid_cells, model_width)], axis=1
    ).astype(bf16)
    (
        grad_position_kernel,
        grad_position_bias,
        grad_early_gain,
        grad_early_shift,
        grad_joint_weight,
        grad_joint_bias,
        grad_small_kernel,
        grad_small_bias,
        grad_middle_kernel,
        grad_middle_bias,
        grad_large_kernel,
        grad_large_bias,
        grad_output_bias,
        grad_late_gain,
        grad_late_shift,
        grad_reduce_bias,
    ) = lax.psum(
        (
            grad_position_kernel,
            grad_position_bias,
            grad_early_gain,
            grad_early_shift,
            grad_joint_weight,
            grad_joint_bias,
            grad_small_kernel,
            grad_small_bias,
            grad_middle_kernel,
            grad_middle_bias,
            grad_large_kernel,
            grad_large_bias,
            grad_output_bias,
            grad_late_gain,
            grad_late_shift,
            grad_reduce_bias,
        ),
        ("dp", "tensor"),
    )
    grad_output_weight, grad_expand_weight, grad_expand_bias, grad_reduce_weight = (
        lax.psum(grad_output_weight.astype(jnp.bfloat16), "dp").astype(jnp.float32),
        lax.psum(grad_expand_weight.astype(jnp.bfloat16), "dp").astype(jnp.float32),
        lax.psum(grad_expand_bias.astype(jnp.bfloat16), "dp").astype(jnp.float32),
        lax.psum(grad_reduce_weight.astype(jnp.bfloat16), "dp").astype(jnp.float32),
    )
    return (
        block_output,
        input_grad,
        grad_position_kernel,
        grad_position_bias,
        grad_early_gain,
        grad_early_shift,
        grad_joint_weight,
        grad_joint_bias,
        grad_small_kernel,
        grad_small_bias,
        grad_middle_kernel,
        grad_middle_bias,
        grad_large_kernel,
        grad_large_bias,
        grad_output_weight,
        grad_output_bias,
        grad_late_gain,
        grad_late_shift,
        grad_expand_weight,
        grad_expand_bias,
        grad_reduce_weight,
        grad_reduce_bias,
    )


def solution(mesh):
    in_specs = (
        P(("dp", "tensor"), None, None),
        P(),
        P(),
        P(),
        P(),
        P(),
        P(),
        P(),
        P(),
        P(),
        P(),
        P(),
        P(),
        P("tensor", None),
        P(),
        P(),
        P(),
        P(None, "tensor"),
        P("tensor"),
        P("tensor", None),
        P(),
        P(("dp", "tensor"), None, None),
    )
    out_specs = (
        P(("dp", "tensor"), None, None),
        P(("dp", "tensor"), None, None),
        P(),
        P(),
        P(),
        P(),
        P(),
        P(),
        P(),
        P(),
        P(),
        P(),
        P(),
        P(),
        P("tensor", None),
        P(),
        P(),
        P(),
        P(None, "tensor"),
        P("tensor"),
        P("tensor", None),
        P(),
    )
    return jax.shard_map(
        per_device, mesh=mesh, in_specs=in_specs, out_specs=out_specs, check_vma=False
    )
```

profile of v0, /device:TPU:0, one launch (start us, length us, event | category | flops | bytes accessed | tf_op | source)
XLA Modules:
  0.0 1119.9 jit_solution(17895176635501025449)
XLA Ops:
  28.4 5.8 reshape.556
  34.3 6.3 all-to-all-start
  48.4 5.8 reshape.558
  54.2 7.2 all-to-all-done
  61.4 4.2 all-to-all-start.2
  69.9 5.9 reshape.554
  76.0 10.0 all-to-all-done.2
  86.0 4.2 all-to-all-start.1
  92.0 7.3 reshape.557
  103.1 8.0 reshape.559
  118.1 8.0 reshape.555
  132.7 4.9 reshape.551
  137.6 4.4 reshape.536
  142.1 6.5 convolution_convert_fusion.4
  154.9 4.5 reshape.537
  159.7 8.4 add_add_fusion.5
  174.9 63.1 %reduce-scatter.4.cloned.1.call-done = bf16[800,512]{1,0:T(8,128)(2,1)} async-done(((bf16[3200,512]{1,0:T(8,128)(2,1)}), bf16[800,512]{1,0:T(8,128)(2,1)}) %reduce-scatter.4.cloned.1.call-update) | async-done | bytes 819216 | tf_op jit(solution)/shard_map/reduce_scatter | solution.py:154
  246.5 61.1 %all-gather.4.cloned.1.call-done = bf16[3200,512]{1,0:T(8,128)(2,1)} async-done(((bf16[800,512]{1,0:T(8,128)(2,1)}), bf16[3200,512]{1,0:T(8,128)(2,1)}) %all-gather.4.cloned.1.call-update) | async-done | bytes 3276816 | tf_op jit(solution)/shard_map/all_gather | solution.py:167
  307.6 6.6 convolution_add_fusion
  314.1 59.3 %all-gather.6.cloned.1.call-done = bf16[3200,512]{1,0:T(8,128)(2,1)} async-done(((bf16[800,512]{1,0:T(8,128)(2,1)}), bf16[3200,512]{1,0:T(8,128)(2,1)}) %all-gather.6.cloned.1.call-update) | async-done | bytes 3276816 | tf_op jit(solution)/shard_map/all_gather | solution.py:186
  373.5 20.2 %fusion.47 = (bf16[512]{0:T(512)(128)(2,1)}, bf16[3200,512]{1,0:T(8,128)(2,1)S(1)}, f32[3200,512]{1,0:T(8,128)}) fusion(f32[3200,512]{1,0:T(8,128)} %convolution_add_fusion, bf16[3200,512]{1,0:T(8,128)(2,1)} %all-gather.6.cloned.1.call-done, bf16[512,512]{1,0:T(8,128)(2,1)} %param.41), kind=kOutput, calls=%fused_computation.363 | convolution fusion | flops 1797324288 | bytes 20186112 | tf_op jit(solution)/shard_map/dot_general | solution.py:188
  399.4 6.8 multiply_convert_fusion
  412.3 47.9 %reduce-scatter.8.cloned.1.call-done = bf16[800,512]{1,0:T(8,128)(2,1)} async-done(((bf16[3200,512]{1,0:T(8,128)(2,1)}), bf16[800,512]{1,0:T(8,128)(2,1)}) %reduce-scatter.8.cloned.1.call-update) | async-done | bytes 819216 | tf_op jit(solution)/shard_map/reduce_scatter | solution.py:192
  462.6 62.2 %reduce-scatter.6.cloned.1.call-done = bf16[800,512]{1,0:T(8,128)(2,1)} async-done(((bf16[3200,512]{1,0:T(8,128)(2,1)}), bf16[800,512]{1,0:T(8,128)(2,1)}) %reduce-scatter.6.cloned.1.call-update) | async-done | bytes 819216 | tf_op jit(solution)/shard_map/reduce_scatter | solution.py:173
  532.5 4.8 convolution_convert_fusion.6
  540.0 55.6 %all-gather.8.cloned.1.call-done = bf16[3200,512]{1,0:T(8,128)(2,1)} async-done(((bf16[800,512]{1,0:T(8,128)(2,1)}), bf16[3200,512]{1,0:T(8,128)(2,1)}) %all-gather.8.cloned.1.call-update) | async-done | bytes 3276816 | tf_op jit(solution)/shard_map/all_gather | solution.py:202
  600.8 5.1 multiply_convert_fusion.1
  610.5 4.2 broadcast_multiply_fusion.2
  615.0 11.5 %broadcast_multiply_fusion.1 = (f32[64,7,7,128]{3,0,2,1:T(8,128)}, f32[64,7,7,128]{3,0,2,1:T(8,128)}, f32[64,7,7,128]{3,0,2,1:T(8,128)}, f32[64,7,7,128]{3,0,2,1...) fusion(f32[64,7,7,128]{3,0,2,1:T(8,128)S(1)} %bitcast.277, ...), kind=kLoop, calls=%fused_computation.225 | loop fusion | flops 7225344 | bytes 30516224 | tf_op jit(solution)/shard_map/transpose(jvp())/mul | solution.py:33
  626.6 11.6 %broadcast_multiply_fusion = (f32[64,7,7,128]{3,0,2,1:T(8,128)}, f32[64,7,7,128]{3,0,2,1:T(8,128)}, f32[64,7,7,128]{3,0,2,1:T(8,128)}, f32[64,7,7,128]{3,0,2,1:T...) fusion(f32[64,7,7,128]{3,0,2,1:T(8,128)S(1)} %bitcast.278, ...), kind=kLoop, calls=%fused_computation.224 | loop fusion | flops 7225344 | bytes 30516224 | tf_op jit(solution)/shard_map/transpose(jvp())/mul | solution.py:33
  641.5 4.4 reshape.543
  649.7 4.4 all-to-all-start.3
  654.1 3.8 fusion.17
  663.3 4.1 reshape.553
  667.5 25.5 %pad_add_fusion = f32[64,13,13,128]{3,0,2,1:T(8,128)} fusion(f32[64,7,7,128]{3,0,2,1:T(8,128)} %get-tuple-element.278, f32[64,7,7,128]{3,0,2,1:T(8,128)} %get-tuple-element.279, f32[64,7,7,128]{3,0,2,1:T(8,128)} %get-tuple-element.280, f32[64,7,7,128]{3,0,2,1:T(8,128)} %get-tuple-element.281, f32[64,7,7,128]{3,0,2,1:T(8,128)} %get-tuple-element.282, ...), kind=kLoop, calls=%fused_computation.70 | loop fusion | flops 58146816 | bytes 74579968 | tf_op jit(solution)/shard_map/transpose(jvp())/add_any | solution.py:33
  693.1 4.8 multiply_reduce_fusion.50
  697.9 4.1 convolution_bitcast_fusion
  701.9 5.3 all-to-all-start.4
  707.2 4.8 pad_add_fusion.8
  715.5 4.4 reshape.545
  729.9 4.2 all-to-all-start.5
  734.2 7.9 multiply_reduce_fusion.52
  762.1 4.2 multiply_reduce_fusion
  784.4 5.3 fusion.41
  790.4 12.9 %psum.157 = bf16[512]{0:T(512)(128)(2,1)S(1)} all-reduce(bf16[512]{0:T(512)(128)(2,1)S(1)} %copy-done.165), channel_id=1, replica_groups=mesh['dp'=8,'tensor'=4] {'dp'}, use_global_device_ids=true, to_apply=%region_99.100 | all-reduce | flops 512 | bytes 2048 | tf_op jit(solution)/shard_map/psum | solution.py:310
  814.2 136.0 %all-reduce.133.cloned.1.call-done = (f32[3,3,512]{2,1,0:T(4,128)}, f32[512]{0:T(512)}, f32[512]{0:T(512)}, f32[512]{0:T(512)}, f32[1024]{0:T(1024)}, /*index=5*...) async-done(((f32[3,3,512]{2,1,0:T(4,128)}, f32[512]{0:T(512)}, ...) | async-done | bytes 100368 | tf_op jit(solution)/shard_map/psum | solution.py:286
  950.2 147.4 %all-reduce.131.cloned.1.call-done = f32[512,1536]{1,0:T(8,128)} async-done(((f32[512,1536]{1,0:T(8,128)}), f32[512,1536]{1,0:T(8,128)}) %all-reduce.131.cloned.1.call-update) | async-done | bytes 3145744 | tf_op jit(solution)/shard_map/psum | solution.py:286
  1102.7 3.8 copy.313
  (526 shorter events, 194.4 us)
Async XLA Ops:
  34.3 27.1 %all-to-all-start = ((bf16[4,2,51200]{2,1,0:T(2,128)(2,1)}), bf16[4,2,51200]{2,1,0:T(2,128)(2,1)S(1)}, u32[]{:S(2)}, u32[]{:S(2)}) async-start(bf16[4,2,51200]{2,1,0:T(2,128)(2,1)} %reshape.556), calls=%async_computation | async-start | bytes 1638400 | tf_op jit(solution)/shard_map/all_to_all | solution.py:106
  61.4 24.6 %all-to-all-start.2 = ((bf16[4,2,51200]{2,1,0:T(2,128)(2,1)}), bf16[4,2,51200]{2,1,0:T(2,128)(2,1)}, u32[]{:S(2)}, u32[]{:S(2)}) async-start(bf16[4,2,51200]{2,1,0:T(2,128)(2,1)} %reshape.558), calls=%async_computation.2 | async-start | bytes 1638400 | tf_op jit(solution)/shard_map/all_to_all | solution.py:105
  76.0 83.4 %copy-start.73 = (f32[128]{0:T(128)}, f32[128]{0:T(128)S(1)}, u32[]{:S(2)}) copy-start(f32[128]{0:T(128)S(1)} %get-tuple-element.359) | copy-start | bytes 1540
  76.0 83.4 %copy-start.75 = (f32[128]{0:T(128)}, f32[128]{0:T(128)S(1)}, u32[]{:S(2)}) copy-start(f32[128]{0:T(128)S(1)} %get-tuple-element.366) | copy-start | bytes 1540
  76.0 83.4 %copy-start.77 = (f32[128]{0:T(128)}, f32[128]{0:T(128)S(1)}, u32[]{:S(2)}) copy-start(f32[128]{0:T(128)S(1)} %get-tuple-element.367) | copy-start | bytes 1540
  76.0 83.4 %copy-start.79 = (f32[128]{0:T(128)}, f32[128]{0:T(128)S(1)}, u32[]{:S(2)}) copy-start(f32[128]{0:T(128)S(1)} %get-tuple-element.368) | copy-start | bytes 1540
  86.0 32.1 %all-to-all-start.1 = ((bf16[4,2,51200]{2,1,0:T(2,128)(2,1)}), bf16[4,2,51200]{2,1,0:T(2,128)(2,1)}, u32[]{:S(2)}, u32[]{:S(2)}) async-start(bf16[4,2,51200]{2,1,0:T(2,128)(2,1)} %reshape.554), calls=%async_computation.1 | async-start | bytes 1638400 | tf_op jit(solution)/shard_map/all_to_all | solution.py:107
  90.2 147.9 %reduce-scatter.4.cloned.1.call-start = ((), (), s32[]{:S(2)}) async-start(), calls=%async_computation.9 | async-start | bytes 4096000 | tf_op jit(solution)/shard_map/reduce_scatter | solution.py:154
  91.2 68.2 %copy-start.81 = (f32[128]{0:T(128)}, f32[128]{0:T(128)S(1)}, u32[]{:S(2)}) copy-start(f32[128]{0:T(128)S(1)} %get-tuple-element.340) | copy-start | bytes 1540
  91.2 68.2 %copy-start.85 = (f32[128]{0:T(128)}, f32[128]{0:T(128)S(1)}, u32[]{:S(2)}) copy-start(f32[128]{0:T(128)S(1)} %get-tuple-element.352) | copy-start | bytes 1540
  91.2 68.2 %copy-start.87 = (f32[128]{0:T(128)}, f32[128]{0:T(128)S(1)}, u32[]{:S(2)}) copy-start(f32[128]{0:T(128)S(1)} %get-tuple-element.353) | copy-start | bytes 1540
  91.2 68.2 %copy-start.89 = (f32[128]{0:T(128)}, f32[128]{0:T(128)S(1)}, u32[]{:S(2)}) copy-start(f32[128]{0:T(128)S(1)} %get-tuple-element.354) | copy-start | bytes 1540
  91.2 68.2 %copy-start.91 = (f32[128]{0:T(128)}, f32[128]{0:T(128)S(1)}, u32[]{:S(2)}) copy-start(f32[128]{0:T(128)S(1)} %get-tuple-element.355) | copy-start | bytes 1540
  91.2 68.2 %copy-start.93 = (f32[128]{0:T(128)}, f32[128]{0:T(128)S(1)}, u32[]{:S(2)}) copy-start(f32[128]{0:T(128)S(1)} %get-tuple-element.356) | copy-start | bytes 1540
  91.2 68.2 %copy-start.95 = (f32[128]{0:T(128)}, f32[128]{0:T(128)S(1)}, u32[]{:S(2)}) copy-start(f32[128]{0:T(128)S(1)} %get-tuple-element.357) | copy-start | bytes 1540
  91.2 68.2 %copy-start.97 = (f32[128]{0:T(128)}, f32[128]{0:T(128)S(1)}, u32[]{:S(2)}) copy-start(f32[128]{0:T(128)S(1)} %get-tuple-element.358) | copy-start | bytes 1540
  91.2 68.2 %copy-start.99 = (f32[128]{0:T(128)}, f32[128]{0:T(128)S(1)}, u32[]{:S(2)}) copy-start(f32[128]{0:T(128)S(1)} %get-tuple-element.341) | copy-start | bytes 1540
  91.2 68.2 %copy-start.101 = (f32[128]{0:T(128)}, f32[128]{0:T(128)S(1)}, u32[]{:S(2)}) copy-start(f32[128]{0:T(128)S(1)} %get-tuple-element.342) | copy-start | bytes 1540
  91.3 68.2 %copy-start.103 = (f32[128]{0:T(128)}, f32[128]{0:T(128)S(1)}, u32[]{:S(2)}) copy-start(f32[128]{0:T(128)S(1)} %get-tuple-element.343) | copy-start | bytes 1540
  91.3 68.2 %copy-start.105 = (f32[128]{0:T(128)}, f32[128]{0:T(128)S(1)}, u32[]{:S(2)}) copy-start(f32[128]{0:T(128)S(1)} %get-tuple-element.344) | copy-start | bytes 1540
  91.3 68.2 %copy-start.107 = (f32[128]{0:T(128)}, f32[128]{0:T(128)S(1)}, u32[]{:S(2)}) copy-start(f32[128]{0:T(128)S(1)} %get-tuple-element.345) | copy-start | bytes 1540
  91.3 68.2 %copy-start.109 = (f32[128]{0:T(128)}, f32[128]{0:T(128)S(1)}, u32[]{:S(2)}) copy-start(f32[128]{0:T(128)S(1)} %get-tuple-element.346) | copy-start | bytes 1540
  91.3 68.2 %copy-start.111 = (f32[128]{0:T(128)}, f32[128]{0:T(128)S(1)}, u32[]{:S(2)}) copy-start(f32[128]{0:T(128)S(1)} %get-tuple-element.347) | copy-start | bytes 1540
  91.9 67.6 %copy-start.83 = (f32[128]{0:T(128)}, f32[128]{0:T(128)S(1)}, u32[]{:S(2)}) copy-start(f32[128]{0:T(128)S(1)} %get-tuple-element.321) | copy-start | bytes 1540
  91.9 67.6 %copy-start.113 = (f32[128]{0:T(128)}, f32[128]{0:T(128)S(1)}, u32[]{:S(2)}) copy-start(f32[128]{0:T(128)S(1)} %get-tuple-element.322) | copy-start | bytes 1540
  92.0 67.6 %copy-start.115 = (f32[128]{0:T(128)}, f32[128]{0:T(128)S(1)}, u32[]{:S(2)}) copy-start(f32[128]{0:T(128)S(1)} %get-tuple-element.330) | copy-start | bytes 1540
  92.0 67.6 %copy-start.117 = (f32[128]{0:T(128)}, f32[128]{0:T(128)S(1)}, u32[]{:S(2)}) copy-start(f32[128]{0:T(128)S(1)} %get-tuple-element.331) | copy-start | bytes 1540
  92.0 67.6 %copy-start.119 = (f32[128]{0:T(128)}, f32[128]{0:T(128)S(1)}, u32[]{:S(2)}) copy-start(f32[128]{0:T(128)S(1)} %get-tuple-element.332) | copy-start | bytes 1540
  92.0 67.6 %copy-start.121 = (f32[128]{0:T(128)}, f32[128]{0:T(128)S(1)}, u32[]{:S(2)}) copy-start(f32[128]{0:T(128)S(1)} %get-tuple-element.333) | copy-start | bytes 1540
  116.5 25.6 %copy-start.38 = (f32[64,2,64]{2,1,0:T(2,128)}, f32[64,2,64]{2,1,0:T(2,128)S(1)}, u32[]{:S(2)}) copy-start(f32[64,2,64]{2,1,0:T(2,128)S(1)} %reshape.552) | copy-start | bytes 98308
  132.7 26.9 %copy-start.1 = (f32[64,49,128]{2,0,1:T(8,128)}, f32[64,49,128]{2,0,1:T(8,128)S(1)}, u32[]{:S(2)}) copy-start(f32[64,49,128]{2,0,1:T(8,128)S(1)} %slice_convert_fusion.1) | copy-start | bytes 4816900
  174.3 133.3 %all-gather.4.cloned.1.call-start = ((), (), s32[]{:S(2)}) async-start(), calls=%async_computation.10 | async-start | bytes 4096000 | tf_op jit(solution)/shard_map/all_gather | solution.py:167
  241.6 131.8 %all-gather.6.cloned.1.call-start = ((), (), s32[]{:S(2)}) async-start(), calls=%async_computation.12 | async-start | bytes 4096000 | tf_op jit(solution)/shard_map/all_gather | solution.py:186
  246.4 213.8 %reduce-scatter.8.cloned.1.call-start = ((), (), s32[]{:S(2)}) async-start(), calls=%async_computation.13 | async-start | bytes 4096000 | tf_op jit(solution)/shard_map/reduce_scatter | solution.py:192
  399.1 125.7 %reduce-scatter.6.cloned.1.call-start = ((), (), s32[]{:S(2)}) async-start(), calls=%async_computation.11 | async-start | bytes 4096000 | tf_op jit(solution)/shard_map/reduce_scatter | solution.py:173
  411.6 184.0 %all-gather.8.cloned.1.call-start = ((), (), s32[]{:S(2)}) async-start(), calls=%async_computation.14 | async-start | bytes 4096000 | tf_op jit(solution)/shard_map/all_gather | solution.py:202
  649.7 52.3 %all-to-all-start.3 = ((bf16[64,50,128]{2,1,0:T(8,128)(2,1)}), bf16[64,50,128]{2,1,0:T(8,128)(2,1)}, u32[]{:S(2)}, u32[]{:S(2)}) async-start(bf16[64,50,128]{2,1,0:T(8,128)(2,1)} %copy.219), calls=%async_computation.6 | async-start | bytes 1835008 | tf_op jit(solution)/shard_map/all_to_all | solution.py:246
  667.4 25.6 %copy-start.74 = (f32[128]{0:T(128)S(1)}, f32[128]{0:T(128)}, u32[]{:S(2)}) copy-start(f32[128]{0:T(128)} %copy-done.73) | copy-start | bytes 1540
  667.4 25.6 %copy-start.76 = (f32[128]{0:T(128)S(1)}, f32[128]{0:T(128)}, u32[]{:S(2)}) copy-start(f32[128]{0:T(128)} %copy-done.75) | copy-start | bytes 1540
  667.4 25.6 %copy-start.78 = (f32[128]{0:T(128)S(1)}, f32[128]{0:T(128)}, u32[]{:S(2)}) copy-start(f32[128]{0:T(128)} %copy-done.77) | copy-start | bytes 1540
  667.4 25.6 %copy-start.80 = (f32[128]{0:T(128)S(1)}, f32[128]{0:T(128)}, u32[]{:S(2)}) copy-start(f32[128]{0:T(128)} %copy-done.79) | copy-start | bytes 1540
  667.4 25.6 %copy-start.82 = (f32[128]{0:T(128)S(1)}, f32[128]{0:T(128)}, u32[]{:S(2)}) copy-start(f32[128]{0:T(128)} %copy-done.81) | copy-start | bytes 1540
  667.5 25.6 %copy-start.84 = (f32[128]{0:T(128)S(1)}, f32[128]{0:T(128)}, u32[]{:S(2)}) copy-start(f32[128]{0:T(128)} %copy-done.83) | copy-start | bytes 1540
  701.9 28.0 %all-to-all-start.4 = ((bf16[64,50,128]{2,1,0:T(8,128)(2,1)}), bf16[64,50,128]{2,1,0:T(8,128)(2,1)}, u32[]{:S(2)}, u32[]{:S(2)}) async-start(bf16[64,50,128]{2,1,0:T(8,128)(2,1)} %reshape.553), calls=%async_computation.7 | async-start | bytes 1835008 | tf_op jit(solution)/shard_map/all_to_all | solution.py:247
  729.9 26.7 %all-to-all-start.5 = ((bf16[64,50,128]{2,1,0:T(8,128)(2,1)}), bf16[64,50,128]{2,1,0:T(8,128)(2,1)}, u32[]{:S(2)}, u32[]{:S(2)}) async-start(bf16[64,50,128]{2,1,0:T(8,128)(2,1)} %copy.229), calls=%async_computation.8 | async-start | bytes 1835008 | tf_op jit(solution)/shard_map/all_to_all | solution.py:248
  734.1 73.1 %all-reduce.135.cloned.1.call-start = ((), (), s32[]{:S(2)}) async-start(), calls=%async_computation.17 | async-start | bytes 2359296 | tf_op jit(solution)/shard_map/psum | solution.py:308
  748.3 201.9 %all-reduce.133.cloned.1.call-start = ((), (), s32[]{:S(2)}) async-start(), calls=%async_computation.16 | async-start | bytes 300032 | tf_op jit(solution)/shard_map/psum | solution.py:286
  784.3 313.2 %all-reduce.131.cloned.1.call-start = ((), (), s32[]{:S(2)}) async-start(), calls=%async_computation.15 | async-start | bytes 6291456 | tf_op jit(solution)/shard_map/psum | solution.py:286
  (145 other events, 685.6 us)
Sparse Core Ops, SparseCore 0:
  174.4 63.6 reduce-scatter.3
  241.8 65.7 all-gather.3
  309.2 64.2 all-gather.5
  399.3 60.9 reduce-scatter.7
  462.4 62.3 reduce-scatter.5
  529.8 65.7 all-gather.7
  748.5 58.7 all-reduce.134
  816.5 133.6 all-reduce.132
  957.2 140.3 all-reduce.130
where the time goes:
time: 1130 us; the launch traced here: 1120 us
  waiting for transfers between devices  657 us (58%)
  local copies, waits for them, and re-layouts  175 us (15%)
  other arithmetic  145 us (13%)
  matrix products  83.9 us (7%)
  starting transfers between devices  29.7 us (3%)
  between operations  16.7 us (1%)
  blocking collectives  12.9 us (1%)
    psum x2, waiting for transfers between devices, per_device(): lax.psum((grad_position_kernel, grad_position_bias, grad_early_gain, grad...  283 us
    unnamed x382, local copies, waits for them, and re-layouts  78.6 us
    reduce_scatter x1, waiting for transfers between devices, per_device(): lax.psum_scatter(jnp.dot(attention_flat, output_weight, preferred_element...  63.1 us
    reduce_scatter x1, waiting for transfers between devices, per_device(): lax.psum_scatter(jnp.dot(lax.slice_in_dim(hidden_low, 0, lax.axis_size('t...  62.2 us
    all_gather x1, waiting for transfers between devices, per_device(): normed_group = lax.all_gather(normed_two, 'tensor', axis=0, tiled=True)  61.1 us
    all_gather x1, waiting for transfers between devices, per_device(): grad_group = lax.all_gather(grad_flat, 'tensor', axis=0, tiled=True)  59.3 us
    all_gather x1, waiting for transfers between devices, per_device(): branch_group = lax.all_gather(grad_branch, 'tensor', axis=0, tiled=True)  55.6 us
    reduce_scatter x1, waiting for transfers between devices, per_device(): lax.psum_scatter(jnp.dot(grad_pre, expand_weight.T, preferred_element_typ...  47.9 us
  transfers between devices with their start and end apart: 15, of which 13 were waited for; matrix products, arithmetic and copies ran while one was open for 19% of the time, Pallas kernels for 0%

commit v1 on v0

--- a/solution.py
+++ b/solution.py
@@ -74,12 +74,16 @@
     bf16 = jnp.bfloat16
     image_count, token_count, model_width = block_input.shape
     row_count = image_count * token_count
-    part_count = lax.axis_size("tensor")
+    part_count = 1
     head_width = model_width // part_count
     heads_here = HEADS // part_count
-    first_chan = lax.axis_index("tensor") * head_width
+    first_chan = 0
     head_scale = HEAD ** (-0.5)
     grid_cells = GRID * GRID
+    output_weight = lax.all_gather(output_weight, "tensor", axis=0, tiled=True)
+    expand_weight = lax.all_gather(expand_weight, "tensor", axis=1, tiled=True)
+    expand_bias = lax.all_gather(expand_bias, "tensor", axis=0, tiled=True)
+    reduce_weight = lax.all_gather(reduce_weight, "tensor", axis=0, tiled=True)
     inputs_f = block_input.astype(f32)
     grid_in = inputs_f[:, 1:].reshape(image_count, GRID, GRID, model_width)
     mixed_grid, pull_position = jax.vjp(
@@ -102,9 +106,9 @@
         (projected[:, 2 * model_width :] + joint_f[model_width:]).astype(bf16).reshape(img_shape)
     )
     query_loc, key_loc, value_loc = (
-        lax.all_to_all(query_img, "tensor", split_axis=2, concat_axis=0, tiled=True),
-        lax.all_to_all(key_img, "tensor", split_axis=2, concat_axis=0, tiled=True),
-        lax.all_to_all(value_img, "tensor", split_axis=2, concat_axis=0, tiled=True),
+        query_img,
+        key_img,
+        value_img,
     )
     group_size = query_loc.shape[0]
     head_shape = (group_size, token_count, heads_here, HEAD)
@@ -151,12 +155,7 @@
         + jnp.concatenate([zero_row, relative], axis=1)
     ).astype(bf16)
     attention_flat = attention.reshape(group_size * token_count, head_width)
-    branch_out = lax.psum_scatter(
-        jnp.dot(attention_flat, output_weight, preferred_element_type=f32).astype(jnp.bfloat16),
-        "tensor",
-        scatter_dimension=0,
-        tiled=True,
-    ).astype(jnp.float32)
+    branch_out = jnp.dot(attention_flat, output_weight, preferred_element_type=f32)
     second_sum = first_sum + branch_out + output_bias.astype(f32)
     normed_two_f, pull_late = jax.vjp(
         layer_norm, second_sum, late_gain.astype(f32), late_shift.astype(f32)
@@ -164,42 +163,31 @@
     normed_two = normed_two_f.astype(bf16)
     exact_gelu = partial(jax.nn.gelu, approximate=False)
     grad_flat = cotangent.reshape(row_count, model_width)
-    normed_group = lax.all_gather(normed_two, "tensor", axis=0, tiled=True)
+    normed_group = normed_two
     pre_gelu = jnp.dot(
         normed_group, expand_weight, preferred_element_type=f32
     ) + expand_bias.astype(f32)
     activated, pull_gelu = jax.vjp(exact_gelu, pre_gelu)
     hidden_low = activated.astype(bf16)
-    feed_out = lax.psum_scatter(
-        jnp.dot(
-            lax.slice_in_dim(hidden_low, 0, lax.axis_size("tensor") * row_count, axis=0),
+    feed_out = jnp.dot(
+            hidden_low,
             reduce_weight,
-            preferred_element_type=f32,
-        ).astype(jnp.bfloat16),
-        "tensor",
-        scatter_dimension=0,
-        tiled=True,
-    ).astype(jnp.float32)
+            preferred_element_type=f32)
     block_output = (second_sum + feed_out + reduce_bias.astype(f32)).astype(bf16).reshape(img_shape)
     grad_out_f = grad_flat.astype(f32)
     grad_reduce_bias = jnp.sum(grad_out_f, axis=0)
-    grad_group = lax.all_gather(grad_flat, "tensor", axis=0, tiled=True)
+    grad_group = grad_flat
     grad_reduce_weight = jnp.dot(hidden_low.T, grad_group, preferred_element_type=f32)
     grad_hidden = jnp.dot(grad_group, reduce_weight.T, preferred_element_type=f32)
     grad_pre = pull_gelu(grad_hidden)[0].astype(bf16)
     grad_expand_bias = jnp.sum(grad_pre.astype(f32), axis=0)
     grad_expand_weight = jnp.dot(normed_group.T, grad_pre, preferred_element_type=f32)
-    grad_normed_two = lax.psum_scatter(
-        jnp.dot(grad_pre, expand_weight.T, preferred_element_type=f32).astype(jnp.bfloat16),
-        "tensor",
-        scatter_dimension=0,
-        tiled=True,
-    ).astype(jnp.float32)
+    grad_normed_two = jnp.dot(grad_pre, expand_weight.T, preferred_element_type=f32)
     grad_second_norm, grad_late_gain, grad_late_shift = pull_late(grad_normed_two)
     grad_second = grad_out_f + grad_second_norm
     grad_branch = grad_second.astype(bf16)
     grad_output_bias = jnp.sum(grad_branch.astype(f32), axis=0)
-    branch_group = lax.all_gather(grad_branch, "tensor", axis=0, tiled=True)
+    branch_group = grad_branch
     grad_output_weight = jnp.dot(attention_flat.T, branch_group, preferred_element_type=f32)
     grad_attention = jnp.dot(branch_group, output_weight.T, preferred_element_type=f32).astype(bf16)
     grad_attention = grad_attention.reshape(group_size, token_count, head_width)
@@ -243,9 +231,9 @@
         )
     ).astype(bf16)
     grad_query_img, grad_key_img, grad_value_img = (
-        lax.all_to_all(grad_query_loc, "tensor", split_axis=0, concat_axis=2, tiled=True),
-        lax.all_to_all(grad_key_loc, "tensor", split_axis=0, concat_axis=2, tiled=True),
-        lax.all_to_all(grad_value_loc, "tensor", split_axis=0, concat_axis=2, tiled=True),
+        grad_query_loc,
+        grad_key_loc,
+        grad_value_loc,
     )
     grad_projected = jnp.concatenate(
         [grad_query_img, grad_key_img, grad_value_img], axis=2
@@ -305,10 +293,15 @@
         ("dp", "tensor"),
     )
     grad_output_weight, grad_expand_weight, grad_expand_bias, grad_reduce_weight = (
-        lax.psum(grad_output_weight.astype(jnp.bfloat16), "dp").astype(jnp.float32),
-        lax.psum(grad_expand_weight.astype(jnp.bfloat16), "dp").astype(jnp.float32),
-        lax.psum(grad_expand_bias.astype(jnp.bfloat16), "dp").astype(jnp.float32),
-        lax.psum(grad_reduce_weight.astype(jnp.bfloat16), "dp").astype(jnp.float32),
+        lax.psum(
+            lax.psum_scatter(part.astype(bf16), "tensor", scatter_dimension=axis, tiled=True), "dp"
+        ).astype(f32)
+        for part, axis in (
+            (grad_output_weight, 0),
+            (grad_expand_weight, 1),
+            (grad_expand_bias, 0),
+            (grad_reduce_weight, 0),
+        )
     )
     return (
         block_output,

time: 1130 us -> 703 us (0.62)
  waiting for transfers between devices: 657 us -> 315 us
  local copies, waits for them, and re-layouts: 175 us -> 104 us
  blocking collectives: 12.9 us -> 54.2 us
  starting transfers between devices: 29.7 us -> 0.32 us
  other arithmetic: 145 us -> 122 us
    all_gather x3 -> x2, waiting for transfers between devices: 176 us -> 0.02 us  [the longest x1 0.02 us: per_device(): expand_weight = lax.all_gather(expand_weight, 'tensor', axis=1, tiled=True)]
    reduce_scatter x3, waiting for transfers between devices: 173 us -> 12.5 us  [per_device(): lax.psum_scatter(part.astype(bf16), 'tensor', scatter_dimension=axis, til...]
    unnamed x382 -> x327, local copies, waits for them, and re-layouts: 78.6 us -> 35.6 us
    all_gather x0 -> x2, blocking collectives: none -> 32.2 us  [the longest x1 18.4 us: per_device(): output_weight = lax.all_gather(output_weight, 'tensor', axis=0, tiled=True)]
    all_to_all x6 -> x0, starting transfers between devices: 28.6 us -> none  [the longest x1 6.32 us: per_device(): lax.all_to_all(key_img, 'tensor', split_axis=2, concat_axis=0, tiled=True)]
    all_to_all x6 -> x0, waiting for transfers between devices: 22.1 us -> none  [the longest x1 9.99 us: per_device(): lax.all_to_all(query_img, 'tensor', split_axis=2, concat_axis=0, tiled=True)]
    all_to_all x6 -> x0, local copies, waits for them, and re-layouts: 14.3 us -> none  [the longest x2 4.51 us: per_device(): lax.all_to_all(query_img, 'tensor', split_axis=2, concat_axis=0, tiled=True)]
    psum x1, waiting for transfers between devices: 1.96 us -> 15.8 us  [per_device(): lax.psum(lax.psum_scatter(part.astype(bf16), 'tensor', scatter_dimension=...]
  transfers between devices with their start and end apart: 15 -> 8, of which waited for: 13 -> 4; matrix products, arithmetic and copies ran while one was open for 19% -> 32% of each run, Pallas kernels for 0% -> 0%
where the time goes in v1:
time: 703 us; the launch traced here: 696 us
  waiting for transfers between devices  315 us (45%)
  other arithmetic  122 us (17%)
  local copies, waits for them, and re-layouts  104 us (15%)
  matrix products  83.2 us (12%)
  blocking collectives  54.2 us (8%)
  between operations  17.2 us (2%)
    psum x2, waiting for transfers between devices, per_device(): lax.psum((grad_position_kernel, grad_position_bias, grad_early_gain, grad...  286 us
    unnamed x327, local copies, waits for them, and re-layouts  35.6 us
    add_any x3, other arithmetic, depthwise(): padded[:, row_tap:row_tap + side_len, col_tap:col_tap + side_len, :]  29.6 us
    mul x4, other arithmetic, depthwise(): padded[:, row_tap:row_tap + side_len, col_tap:col_tap + side_len, :]  25.8 us
    reduce_sum x5, other arithmetic, depthwise(): padded[:, row_tap:row_tap + side_len, col_tap:col_tap + side_len, :]  24 us
    dot_general x1, matrix products, per_device(): jnp.dot(normed_group, expand_weight, preferred_element_type=f32)  19.9 us
    all_gather x1, blocking collectives, per_device(): output_weight = lax.all_gather(output_weight, 'tensor', axis=0, tiled=True)  18.4 us
    psum x1, waiting for transfers between devices, per_device(): lax.psum(lax.psum_scatter(part.astype(bf16), 'tensor', scatter_dimension=...  15.8 us
  transfers between devices with their start and end apart: 8, of which 4 were waited for; matrix products, arithmetic and copies ran while one was open for 32% of the time, Pallas kernels for 0%

profile of v1, /device:TPU:0, one launch (start us, length us, event | category | flops | bytes accessed | tf_op | source)
XLA Modules:
  0.0 696.0 jit_solution(8002488308081360675)
XLA Ops:
  16.3 2.6 convert_element_type.153
  21.2 3.6 copy.129
  37.9 13.8 %all-gather = bf16[4,1,512]{2,1,0:T(2,128)(2,1)S(1)} all-gather(bf16[1,1,512]{2,1,0:T(2,128)(2,1)S(1)} %reshape.542), channel_id=1, replica_groups=mesh['dp'=8,'tensor'=4] {'tensor'}, dimensions={0}, use_global_device_ids=true | all-gather | bytes 5120 | tf_op jit(solution)/shard_map/all_gather | solution.py:85
  52.3 18.4 %all_gather.12 = bf16[512,512]{1,0:T(8,128)(2,1)} all-gather(bf16[128,512]{1,0:T(8,128)(2,1)S(1)} %copy-done.57), channel_id=1, replica_groups=mesh['dp'=8,'tensor'=4] {'tensor'}, dimensions={0}, use_global_device_ids=true | all-gather | bytes 655360 | tf_op jit(solution)/shard_map/all_gather | solution.py:83
  72.5 2.5 reshape_reshape.12
  84.2 2.3 copy.136
  86.8 3.9 reshape.524
  91.0 8.8 %add_add_fusion.5 = f32[16,7,7,512]{3,0,2,1:T(8,128)S(1)} fusion(f32[16,7,7,512]{3,0,2,1:T(8,128)S(1)} %bitcast.194, f32[512]{0:T(512)S(1)} %maximum_convert_fusion, f32[512]{0:T(512)S(1)} %bitcast.271, f32[512]{0:T(512)S(1)} %bitcast.289, f32[512]{0:T(512)S(1)} %bitcast.309, f32[512]{0:T(512)S(1)} %bitcast.311, f32[512]{0:T(512)S(1)} %bitcast.313, ...), kind=kLoop, calls=%fused_computation.203 | loop fusion | flops 39337984 | bytes 3313664 | tf_op jit(solution)/shard_map/jvp()/add | solution.py:136
  103.9 2.5 fusion.59
  107.2 19.9 %multiply_convert_fusion = (bf16[800,2048]{1,0:T(8,128)(2,1)}, f32[800,2048]{1,0:T(8,128)}, f32[800,2048]{1,0:T(8,128)}) fusion(f32[2048]{0:T(1024)S(1)} %bitcast.374, bf16[512,2048]{1,0:T(8,128)(2,1)} %all-gather.4.cloned.1.call-done, f32[800,512]{1,0:T(8,128)S(1)} %get-tuple-element.360, f32[512]{0:T(512)S(1)} %convert_element_type.170, ...), kind=kOutput, calls=%fused_computation.52 | convolution fusion | flops 1787904000 | bytes 20138240 | tf_op jit(solution)/shard_map/dot_general | solution.py:167
  127.1 9.4 %fusion.60 = (bf16[2048]{0:T(1024)(128)(2,1)S(1)}, bf16[800,2048]{1,0:T(8,128)(2,1)S(1)}) fusion(f32[800,2048]{1,0:T(8,128)} %get-tuple-element.228, bf16[800,512]{1,0:T(8,128)(2,1)} %reshape.531, bf16[2048,512]{1,0:T(8,128)(2,1)} %all-gather.6.cloned.1.call-done, f32[800,2048]{1,0:T(8,128)} %get-tuple-element.361, f32[2048]{0:T(1024)S(1)} %bitcast.375), kind=kOutput, calls=%fused_computation.317 | convolution fusion | flops 1703933952 | bytes 19312640 | tf_op jit(solution)/shard_map/dot_general | solution.py:181
  138.4 3.9 convolution_convert_fusion.1
  142.2 5.5 multiply_reduce_fusion
  156.1 3.6 reshape_reshape.15
  159.7 4.1 multiply_convert_fusion.1
  163.8 3.1 multiply_bitcast_fusion
  170.5 4.4 broadcast_multiply_fusion.2
  174.8 9.6 %broadcast_multiply_fusion.1 = (f32[16,7,7,512]{3,0,2,1:T(8,128)}, f32[16,7,7,512]{3,0,2,1:T(8,128)}, f32[16,7,7,512]{3,0,2,1:T(8,128)}, f32[16,7,7,512]{3,0,2,1...) fusion(f32[16,7,7,512]{3,0,2,1:T(8,128)S(1)} %bitcast.189, ...), kind=kLoop, calls=%fused_computation.222 | loop fusion | flops 7225344 | bytes 30543872 | tf_op jit(solution)/shard_map/transpose(jvp())/mul | solution.py:33
  184.6 5.2 convolution_bitcast_fusion.1
  189.7 3.1 fusion.15
  192.8 2.3 copy.142
  195.2 3.9 reshape.532
  199.1 4.4 copy.148
  203.5 3.9 reshape.534
  207.4 9.8 %broadcast_multiply_fusion = (f32[16,7,7,512]{3,0,2,1:T(8,128)}, f32[16,7,7,512]{3,0,2,1:T(8,128)}, f32[16,7,7,512]{3,0,2,1:T(8,128)}, f32[16,7,7,512]{3,0,2,1:T...) fusion(f32[16,7,7,512]{3,0,2,1:T(8,128)S(1)} %bitcast.190, ...), kind=kLoop, calls=%fused_computation.221 | loop fusion | flops 7225344 | bytes 30543872 | tf_op jit(solution)/shard_map/transpose(jvp())/mul | solution.py:33
  217.3 26.5 %pad_add_fusion = f32[16,13,13,512]{3,0,2,1:T(8,128)} fusion(f32[16,7,7,512]{3,0,2,1:T(8,128)} %get-tuple-element.252, f32[16,7,7,512]{3,0,2,1:T(8,128)} %get-tuple-element.253, f32[16,7,7,512]{3,0,2,1:T(8,128)} %get-tuple-element.254, f32[16,7,7,512]{3,0,2,1:T(8,128)} %get-tuple-element.255, f32[16,7,7,512]{3,0,2,1:T(8,128)} %get-tuple-element.256, ...), kind=kLoop, calls=%fused_computation.66 | loop fusion | flops 58146816 | bytes 74579968 | tf_op jit(solution)/shard_map/transpose(jvp())/add_any | solution.py:33
  246.9 3.5 convert_element_type.184
  250.4 6.3 multiply_reduce_fusion.52
  256.8 2.4 pad_add_fusion.8
  261.7 2.9 copy.149
  264.6 4.3 reshape.537
  269.0 4.7 multiply_reduce_fusion.1
  276.5 3.7 convolution_convert_fusion
  280.3 3.7 add_add_fusion.2
  284.0 3.1 reshape.538
  287.1 10.8 %multiply_reduce_fusion.53 = (f32[512]{0:T(512)S(1)}, f32[512]{0:T(512)S(1)}, f32[512]{0:T(512)S(1)}, f32[512]{0:T(512)S(1)}, f32[512]{0:T(512)S(1)}, /*index=5*...) fusion(f32[16,7,7,512]{3,0,2,1:T(8,128)S(1)} %bitcast.192, ...), kind=kLoop, calls=%fused_computation.192 | loop fusion | flops 14441472 | bytes 3248128 | tf_op jit(solution)/shard_map/transpose(jvp())/reduce_sum | solution.py:33
  297.9 2.2 multiply_reduce_fusion.54
  306.5 3.6 multiply_reduce_fusion.63
  310.2 12.5 %reduce-scatter.8.cloned.1.call-done = bf16[512,512]{1,0:T(8,128)(2,1)} async-done(((bf16[2048,512]{1,0:T(8,128)(2,1)}), bf16[512,512]{1,0:T(8,128)(2,1)}) %reduce-scatter.8.cloned.1.call-update) | async-done | bytes 524304 | tf_op jit(solution)/shard_map/reduce_scatter | solution.py:297
  327.1 5.3 convolution_bitcast_fusion
  335.3 9.8 %all-reduce.125 = bf16[2048]{0:T(1024)(128)(2,1)S(1)} all-reduce(bf16[2048]{0:T(1024)(128)(2,1)S(1)} %get-tuple-element.364), channel_id=4, replica_groups=mesh['dp'=8,'tensor'=4] {'tensor'}, use_global_device_ids=true, to_apply=%region_98.99.clone | all-reduce | flops 2048 | bytes 8192
  345.2 12.2 %psum.157 = bf16[512]{0:T(512)(128)(2,1)S(1)} all-reduce(bf16[512]{0:T(512)(128)(2,1)S(1)} %dynamic-slice.1), channel_id=1, replica_groups=mesh['dp'=8,'tensor'=4] {'dp'}, use_global_device_ids=true, to_apply=%region_99.100 | all-reduce | flops 512 | bytes 2048 | tf_op jit(solution)/shard_map/psum | solution.py:296
  358.0 5.4 add_convert_fusion.4
  367.0 15.8 %all-reduce.136.cloned.1.call-done = (bf16[128,512]{1,0:T(8,128)(2,1)}, bf16[512,512]{1,0:T(8,128)(2,1)}, bf16[512,512]{1,0:T(8,128)(2,1)}) async-done(((bf16[128,512]{1,0:T(8,128)(2,1)}, bf16[512,512]{1,0:T(8,128)(2,1)}, bf16[512,512]{1,0:T(8,128)(2,1)}), (bf16[128,512]{1,0:T(8,128)(2,1)}, bf16[512,512]{1,0:T(8,128)(2,1)}, bf16[512,512]{1,0:T(8,128)(2,1)})) %all-reduce.136.cloned.1.call-update) | async-done | bytes 1179664 | tf_op jit(solution)/shard_map/psum | solution.py:296
  384.5 2.1 convert_element_type.193
  387.7 138.2 %all-reduce.134.cloned.1.call-done = (f32[3,3,512]{2,1,0:T(4,128)}, f32[512]{0:T(512)}, f32[512]{0:T(512)}, f32[512]{0:T(512)}, f32[1024]{0:T(1024)}, /*index=5*...) async-done(((f32[3,3,512]{2,1,0:T(4,128)}, f32[512]{0:T(512)}, ...) | async-done | bytes 100368 | tf_op jit(solution)/shard_map/psum | solution.py:274
  525.9 147.3 %all-reduce.132.cloned.1.call-done = f32[512,1536]{1,0:T(8,128)} async-done(((f32[512,1536]{1,0:T(8,128)}), f32[512,1536]{1,0:T(8,128)}) %all-reduce.132.cloned.1.call-update) | async-done | bytes 3145744 | tf_op jit(solution)/shard_map/psum | solution.py:274
  678.4 3.8 copy.220
  (435 shorter events, 93.9 us)
Async XLA Ops:
  7.2 19.3 %copy-start = (bf16[512,1536]{1,0:T(8,128)(2,1)S(1)}, bf16[512,1536]{1,0:T(8,128)(2,1)}, u32[]{:S(2)}) copy-start(bf16[512,1536]{1,0:T(8,128)(2,1)} %param.27) | copy-start | bytes 4718596
  7.2 99.7 %all-gather.4.cloned.1.call-start = ((), (), s32[]{:S(2)}) async-start(), calls=%async_computation.3 | async-start | bytes 2621440 | tf_op jit(solution)/shard_map/all_gather | solution.py:84
  8.0 5.2 copy-start.25
  8.0 119.2 %all-gather.6.cloned.1.call-start = ((), (), s32[]{:S(2)}) async-start(), calls=%async_computation.4 | async-start | bytes 2621440 | tf_op jit(solution)/shard_map/all_gather | solution.py:86
  8.7 301.4 %reduce-scatter.4.cloned.1.call-start = ((), (), s32[]{:S(2)}) async-start(), calls=%async_computation.6 | async-start | bytes 655360 | tf_op jit(solution)/shard_map/reduce_scatter | solution.py:297
  9.6 81.1 %copy-start.84 = (f32[1,1,512]{2,1,0:T(1,128)}, f32[1,1,512]{2,1,0:T(1,128)S(1)}, u32[]{:S(2)}) copy-start(f32[1,1,512]{2,1,0:T(1,128)S(1)} %get-tuple-element.333) | copy-start | bytes 6148
  9.7 81.1 %copy-start.86 = (f32[1,1,512]{2,1,0:T(1,128)}, f32[1,1,512]{2,1,0:T(1,128)S(1)}, u32[]{:S(2)}) copy-start(f32[1,1,512]{2,1,0:T(1,128)S(1)} %get-tuple-element.341) | copy-start | bytes 6148
  9.7 81.1 %copy-start.88 = (f32[1,1,512]{2,1,0:T(1,128)}, f32[1,1,512]{2,1,0:T(1,128)S(1)}, u32[]{:S(2)}) copy-start(f32[1,1,512]{2,1,0:T(1,128)S(1)} %get-tuple-element.342) | copy-start | bytes 6148
  9.7 81.1 %copy-start.90 = (f32[1,1,512]{2,1,0:T(1,128)}, f32[1,1,512]{2,1,0:T(1,128)S(1)}, u32[]{:S(2)}) copy-start(f32[1,1,512]{2,1,0:T(1,128)S(1)} %get-tuple-element.343) | copy-start | bytes 6148
  10.3 80.4 %copy-start.92 = (f32[1,1,512]{2,1,0:T(1,128)}, f32[1,1,512]{2,1,0:T(1,128)S(1)}, u32[]{:S(2)}) copy-start(f32[1,1,512]{2,1,0:T(1,128)S(1)} %get-tuple-element.314) | copy-start | bytes 6148
  11.0 79.8 %copy-start.94 = (f32[1,1,512]{2,1,0:T(1,128)}, f32[1,1,512]{2,1,0:T(1,128)S(1)}, u32[]{:S(2)}) copy-start(f32[1,1,512]{2,1,0:T(1,128)S(1)} %get-tuple-element.295) | copy-start | bytes 6148
  13.2 5.9 copy-start.55
  16.2 10.2 %copy-start.123 = (f32[800]{0:T(1024)}, f32[800]{0:T(1024)S(1)}, u32[]{:S(2)}) copy-start(f32[800]{0:T(1024)S(1)} %div.47) | copy-start | bytes 9604
  19.0 7.4 %copy-start.128 = (f32[512]{0:T(512)}, f32[512]{0:T(512)S(1)}, u32[]{:S(2)}) copy-start(f32[512]{0:T(512)S(1)} %convert_element_type.156) | copy-start | bytes 6148
  19.0 7.4 %copy-start.134 = (f32[512]{0:T(512)}, f32[512]{0:T(512)S(1)}, u32[]{:S(2)}) copy-start(f32[512]{0:T(512)S(1)} %convert_element_type.157) | copy-start | bytes 6148
  20.6 5.8 copy-start.125
  33.5 18.8 %copy-start.57 = (bf16[128,512]{1,0:T(8,128)(2,1)S(1)}, bf16[128,512]{1,0:T(8,128)(2,1)}, u32[]{:S(2)}) copy-start(bf16[128,512]{1,0:T(8,128)(2,1)} %param.35) | copy-start | bytes 393220
  33.5 37.2 %copy-start.42 = (bf16[16,50,512]{2,1,0:T(8,128)(2,1)S(1)}, bf16[16,50,512]{2,1,0:T(8,128)(2,1)}, u32[]{:S(2)}) copy-start(bf16[16,50,512]{2,1,0:T(8,128)(2,1)} %copy.140) | copy-start | bytes 2457604
  80.8 10.0 %copy-start.1 = (f32[16,49,512]{2,0,1:T(8,128)}, f32[16,49,512]{2,0,1:T(8,128)S(1)}, u32[]{:S(2)}) copy-start(f32[16,49,512]{2,0,1:T(8,128)S(1)} %copy_convert_fusion) | copy-start | bytes 4816900
  91.0 8.9 %copy-start.20 = (bf16[16,49,512]{2,1,0:T(8,128)(2,1)S(1)}, bf16[16,49,512]{2,1,0:T(8,128)(2,1)}, u32[]{:S(2)}) copy-start(bf16[16,49,512]{2,1,0:T(8,128)(2,1)} %slice.530) | copy-start | bytes 2408452
  106.5 41.3 %copy-start.3 = (f32[800,512]{1,0:T(8,128)}, f32[800,512]{1,0:T(8,128)S(1)}, u32[]{:S(2)}) copy-start(f32[800,512]{1,0:T(8,128)S(1)} %get-tuple-element.360) | copy-start | bytes 4915204
  184.5 125.7 %reduce-scatter.6.cloned.1.call-start = ((), (), s32[]{:S(2)}) async-start(), calls=%async_computation.7 | async-start | bytes 2621440 | tf_op jit(solution)/shard_map/reduce_scatter | solution.py:297
  184.5 5.2 copy-start.29
  184.6 5.2 copy-start.52
  217.2 105.5 %reduce-scatter.8.cloned.1.call-start = ((), (), s32[]{:S(2)}) async-start(), calls=%async_computation.8 | async-start | bytes 2621440 | tf_op jit(solution)/shard_map/reduce_scatter | solution.py:297
  217.2 26.6 %copy-start.7 = (bf16[16,50,8,64]{3,2,1,0:T(8,128)(2,1)S(1)}, bf16[16,50,8,64]{3,2,1,0:T(8,128)(2,1)}, u32[]{:S(2)}) copy-start(bf16[16,50,8,64]{3,2,1,0:T(8,128)(2,1)} %copy-done.5) | copy-start | bytes 2457604
  217.3 26.6 %copy-start.41 = (f32[16,8,64,50]{2,3,1,0:T(8,128)S(1)}, f32[16,8,64,50]{2,3,1,0:T(8,128)}, u32[]{:S(2)}) copy-start(f32[16,8,64,50]{2,3,1,0:T(8,128)} %fusion.15) | copy-start | bytes 4915204
  268.9 4.8 copy-start.63
  268.9 4.8 copy-start.9
  280.2 102.5 %all-reduce.136.cloned.1.call-start = ((), (), s32[]{:S(2)}) async-start(), calls=%async_computation.10 | async-start | bytes 2359296 | tf_op jit(solution)/shard_map/psum | solution.py:296
  287.1 10.8 %copy-start.2 = (f32[16,49,512]{2,0,1:T(8,128)S(1)}, f32[16,49,512]{2,0,1:T(8,128)}, u32[]{:S(2)}) copy-start(f32[16,49,512]{2,0,1:T(8,128)} %copy-done.1) | copy-start | bytes 4816900
  306.5 20.6 %copy-start.64 = (f32[16,50]{0,1:T(8,128)S(1)}, f32[16,50]{0,1:T(8,128)}, u32[]{:S(2)}) copy-start(f32[16,50]{0,1:T(8,128)} %copy.152) | copy-start | bytes 9604
  310.1 17.0 %copy-start.15 = (f32[16,7,7,512]{3,0,2,1:T(8,128)S(1)}, f32[16,7,7,512]{3,0,2,1:T(8,128)}, u32[]{:S(2)}) copy-start(f32[16,7,7,512]{3,0,2,1:T(8,128)} %copy-done.14) | copy-start | bytes 4816900
  310.1 17.0 %copy-start.56 = (f32[16,1,512]{2,0,1:T(8,128)S(1)}, f32[16,1,512]{2,0,1:T(8,128)}, u32[]{:S(2)}) copy-start(f32[16,1,512]{2,0,1:T(8,128)} %copy-done.55) | copy-start | bytes 98308
  310.1 17.0 %copy-start.59 = (f32[16,50]{0,1:T(8,128)S(1)}, f32[16,50]{0,1:T(8,128)}, u32[]{:S(2)}) copy-start(f32[16,50]{0,1:T(8,128)} %copy-done.58) | copy-start | bytes 9604
  310.1 17.0 %copy-start.135 = (f32[512]{0:T(512)S(1)}, f32[512]{0:T(512)}, u32[]{:S(2)}) copy-start(f32[512]{0:T(512)} %copy-done.134) | copy-start | bytes 6148
  322.7 203.3 %all-reduce.134.cloned.1.call-start = ((), (), s32[]{:S(2)}) async-start(), calls=%async_computation.9 | async-start | bytes 300032 | tf_op jit(solution)/shard_map/psum | solution.py:274
  327.0 346.2 %all-reduce.132.cloned.1.call-start = ((), (), s32[]{:S(2)}) async-start(), calls=%async_computation.5 | async-start | bytes 6291456 | tf_op jit(solution)/shard_map/psum | solution.py:274
  332.4 25.6 %copy-start.4 = (f32[800,512]{1,0:T(8,128)S(1)}, f32[800,512]{1,0:T(8,128)}, u32[]{:S(2)}) copy-start(f32[800,512]{1,0:T(8,128)} %copy-done.3) | copy-start | bytes 4915204
  678.4 5.0 copy-start.150
  678.4 5.6 copy-start.61
  678.4 6.2 copy-start.146
  678.4 6.7 copy-start.60
  678.4 7.3 %copy-start.145 = (f32[192]{0:T(256)S(1)}, f32[192]{0:T(256)}, u32[]{:S(2)}) copy-start(f32[192]{0:T(256)} %get-tuple-element.381) | copy-start | bytes 2308
  678.4 7.9 %copy-start.139 = (f32[512]{0:T(512)S(1)}, f32[512]{0:T(512)}, u32[]{:S(2)}) copy-start(f32[512]{0:T(512)} %get-tuple-element.383) | copy-start | bytes 6148
  678.4 8.5 %copy-start.138 = (f32[512]{0:T(512)S(1)}, f32[512]{0:T(512)}, u32[]{:S(2)}) copy-start(f32[512]{0:T(512)} %get-tuple-element.384) | copy-start | bytes 6148
  678.4 9.0 %copy-start.137 = (f32[512]{0:T(512)S(1)}, f32[512]{0:T(512)}, u32[]{:S(2)}) copy-start(f32[512]{0:T(512)} %get-tuple-element.385) | copy-start | bytes 6148
  678.4 9.6 %copy-start.136 = (f32[512]{0:T(512)S(1)}, f32[512]{0:T(512)}, u32[]{:S(2)}) copy-start(f32[512]{0:T(512)} %get-tuple-element.389) | copy-start | bytes 6148
  (113 other events, 304.5 us)
Sparse Core Ops, SparseCore 0:
  9.6 51.7 all-gather.3
  62.9 44.0 all-gather.5
  184.6 19.9 reduce-scatter.3
  217.3 42.1 reduce-scatter.5
  280.4 42.2 reduce-scatter.7
  326.0 56.7 all-reduce.135
  392.0 133.8 all-reduce.133
  532.9 140.3 all-reduce.131

commit v2 on v1

v2 whole, which is shorter than its diff:
```python
from functools import partial

import jax
import jax.numpy as jnp
from jax import lax
from jax.experimental import pallas as pl
from jax.experimental.pallas import tpu as pltpu
from jax.sharding import PartitionSpec as P

HEADS = 8
HEAD = 64
GRID = 7
CELLS = GRID * GRID
NORM_EPS = 1e-06
SCALE = HEAD**-0.5
LANES = 128
GROUP = 256
PAD_TOK = 64
VMEM_BYTES = 56 * 1024 * 1024

f32 = jnp.float32
bf16 = jnp.bfloat16

ROW_POS_BIAS, ROW_EARLY_GAIN, ROW_EARLY_SHIFT, ROW_BIAS_Q, ROW_BIAS_V = 0, 1, 2, 3, 4
ROW_BIAS_ALL, ROW_OUT_BIAS, ROW_LATE_GAIN, ROW_LATE_SHIFT, ROW_REDUCE_BIAS = 5, 6, 7, 8, 9
ROW_POS_KERNEL, ROW_KERNEL_ALL = 10, 19
PARAM_ROWS = 72

OUT_POS_KERNEL, OUT_KERNEL_ALL = 0, 9
OUT_POS_BIAS, OUT_EARLY_GAIN, OUT_EARLY_SHIFT, OUT_BIAS_Q, OUT_BIAS_V, OUT_BIAS_ALL = 58, 59, 60, 61, 62, 63
SMALL_ROWS = 64
LATE_GAIN, LATE_SHIFT, LATE_OUT_BIAS, LATE_REDUCE_BIAS, LATE_EXPAND_BIAS = 0, 1, 2, 3, 4


def lane(tile):
    if isinstance(tile, int):
        return slice(tile * LANES, (tile + 1) * LANES)
    return pl.ds(pl.multiple_of(tile * LANES, LANES), LANES)


def taps(extent):
    return range(extent)


def columns(shift):
    return range(max(0, -shift), min(GRID, GRID - shift))


def depthwise_rows(get_row, get_weight, extent, flip, emit):
    margin = extent // 2
    for i in range(GRID):
        total = [None] * GRID
        for a in range(extent):
            r = i + a - margin
            if not 0 <= r < GRID:
                continue
            row = get_row(r)
            for b in range(extent):
                weight = get_weight((extent - 1 - a, extent - 1 - b) if flip else (a, b))
                for j in columns(b - margin):
                    term = row[j + b - margin] * weight
                    total[j] = term if total[j] is None else total[j] + term
        emit(i, total)


def kernel_grads(get_left, get_right, extent, emit):
    margin = extent // 2
    for a in range(extent):
        total = [None] * extent
        for i in range(GRID):
            r = i + a - margin
            if not 0 <= r < GRID:
                continue
            left, right = get_left(i), get_right(r)
            for b in range(extent):
                for j in columns(b - margin):
                    term = left[j] * right[j + b - margin]
                    total[b] = term if total[b] is None else total[b] + term
        for b in range(extent):
            emit(a, b, total[b])


def cell_rows(images, cell, count=1):
    return slice((1 + cell) * images, (1 + cell + count) * images)


def grid_row(ref, tile, images, i):
    block = ref[tile, cell_rows(images, i * GRID, GRID), :]
    return [block[j * images : (j + 1) * images] for j in range(GRID)]


def full_tap(extent, a, b):
    extra = (GRID - extent) // 2
    return ROW_KERNEL_ALL + (a + extra) * GRID + b + extra


def tile_extents(body):
    body(0, 3)
    body(1, 5)

    def rest(tile, carry):
        body(tile, 7)
        return carry

    lax.fori_loop(2, 4, rest, 0)


def normalise(block, gain, shift):
    centre = jnp.mean(block, axis=-1, keepdims=True)
    centred = block - centre
    spread = jnp.mean(centred * centred, axis=-1, keepdims=True)
    scale = lax.rsqrt(spread + NORM_EPS)
    return centred * scale, scale


def normalise_back(grad, gain, unit, scale):
    scaled = grad * gain
    mean_one = jnp.mean(scaled, axis=-1, keepdims=True)
    mean_two = jnp.mean(scaled * unit, axis=-1, keepdims=True)
    return (scaled - mean_one - unit * mean_two) * scale


def fold_rows(block):
    return jnp.sum(block.reshape(block.shape[0] // 8, 8, block.shape[1]), axis=0)


def dot(left, right, left_dim=1, right_dim=0):
    return lax.dot_general(
        left, right, (((left_dim,), (right_dim,)), ((), ())), preferred_element_type=f32
    )


def head_of(rows, columns_):
    return lax.broadcasted_iota(jnp.int32, (rows, columns_), 1) // HEAD


def to_tokens(images, tokens, source, target):
    for tile in range(4):
        for b in range(images):
            target[tile, pl.ds(b, tokens, stride=images), :] = source(b, tile)


def compact_context(full):
    heads = head_of(HEAD, GROUP)
    total = jnp.zeros((HEAD, GROUP), f32)
    for h in range(GROUP // HEAD):
        total = jnp.where(heads == h, full[h * HEAD : (h + 1) * HEAD, :], total)
    return total.astype(bf16)


def spread_context(compact):
    heads = head_of(HEAD, GROUP)
    wide = compact.astype(f32)
    return jnp.concatenate(
        [jnp.where(heads == h, wide, 0.0).astype(bf16) for h in range(GROUP // HEAD)], axis=0
    )


def attention_forward(
    images, tokens, x_ref, prm_ref, wj_ref,
    xt_ref, x1_ref, h1_ref, q_ref, v_ref, ks_ref, conv_ref, qi_ref, ki_ref, vi_ref, ctx_ref, att_ref,
    fac_ref,
):
    rows = images * tokens
    prm = lambda row, tile: prm_ref[row : row + 1, lane(tile)]
    to_tokens(images, tokens, lambda b, t: x_ref[b, :, lane(t)].astype(f32), xt_ref)

    def position(tile, carry):
        x1_ref[0:images, lane(tile)] = xt_ref[tile, 0:images, :]
        bias = prm(ROW_POS_BIAS, tile)

        def emit(i, total):
            own = grid_row(xt_ref, tile, images, i)
            for j in range(GRID):
                x1_ref[cell_rows(images, i * GRID + j), lane(tile)] = own[j] + total[j] + bias

        depthwise_rows(
            lambda r: grid_row(xt_ref, tile, images, r),
            lambda ab: prm(ROW_POS_KERNEL + ab[0] * 3 + ab[1], tile),
            3, False, emit,
        )
        return carry

    lax.fori_loop(0, 4, position, 0)
    gain = prm_ref[ROW_EARLY_GAIN : ROW_EARLY_GAIN + 1, :]
    shift = prm_ref[ROW_EARLY_SHIFT : ROW_EARLY_SHIFT + 1, :]
    step = 80

    def norm(k, carry):
        at = pl.ds(pl.multiple_of(k * step, step), step)
        unit, _ = normalise(x1_ref[at, :], gain, shift)
        h1_ref[at, :] = (unit * gain + shift).astype(bf16)
        return carry

    lax.fori_loop(0, rows // step, norm, 0)

    width = 4 * LANES
    query = (dot(h1_ref[...], wj_ref[:, :width]) + prm_ref[ROW_BIAS_Q : ROW_BIAS_Q + 1, :]).astype(bf16).astype(f32)
    for tile in range(4):
        q_ref[tile] = query[:, lane(tile)]
    value = (dot(h1_ref[...], wj_ref[:, 2 * width :]) + prm_ref[ROW_BIAS_V : ROW_BIAS_V + 1, :]).astype(bf16).astype(f32)
    for tile in range(4):
        v_ref[tile] = value[:, lane(tile)]
    keys = dot(h1_ref[...], wj_ref[:, width : 2 * width]).astype(bf16).astype(f32)
    for tile in range(4):
        ks_ref[tile] = keys[:, lane(tile)]

    def soften(tile, carry):
        at = lambda n: slice(n * images, (n + 1) * images)
        top = ks_ref[tile, at(0), :]
        for n in range(1, tokens):
            top = jnp.maximum(top, ks_ref[tile, at(n), :])
        total = jnp.zeros_like(top)
        for n in range(tokens):
            e = jnp.exp(ks_ref[tile, at(n), :] - top)
            ks_ref[tile, at(n), :] = e
            total = total + e
        scale = 1.0 / total
        for n in range(tokens):
            ks_ref[tile, at(n), :] = ks_ref[tile, at(n), :] * scale
        return carry

    lax.fori_loop(0, 4, soften, 0)

    def relative(tile, extent):
        conv_ref[tile, 0:images, :] = jnp.zeros((images, LANES), f32)
        bias = prm(ROW_BIAS_ALL, tile)

        def emit(i, total):
            for j in range(GRID):
                conv_ref[tile, cell_rows(images, i * GRID + j), :] = total[j] + bias

        depthwise_rows(
            lambda r: grid_row(v_ref, tile, images, r),
            lambda ab: prm(full_tap(extent, *ab), tile),
            extent, False, emit,
        )

    tile_extents(relative)

    def image(b, carry):
        for source, target in ((q_ref, qi_ref), (ks_ref, ki_ref), (v_ref, vi_ref)):
            target[b, 48:PAD_TOK, :] = jnp.zeros((PAD_TOK - 48, width), bf16)
            for tile in range(4):
                target[b, 0:tokens, lane(tile)] = source[tile, pl.ds(b, tokens, stride=images), :].astype(bf16)
        for g in range(2):
            at = slice(g * GROUP, (g + 1) * GROUP)
            compact = compact_context(dot(ki_ref[b, :, at], vi_ref[b, :, at], 0, 0))
            ctx_ref[b, :, at] = compact
            out = dot(qi_ref[b, :, at], spread_context(compact)) * SCALE
            for t in range(2):
                fac_ref[2 * g + t, pl.ds(b, tokens, stride=images), :] = out[0:tokens, lane(t)]
        return carry

    lax.fori_loop(0, images, image, 0)

    def combine(tile, carry):
        att_ref[:, lane(tile)] = (fac_ref[tile] + q_ref[tile] * conv_ref[tile]).astype(bf16)
        return carry

    lax.fori_loop(0, 4, combine, 0)


def feed_forward(
    images, tokens, chunks, att_ref, x1_ref, prm_ref, eb_ref, wo_ref, we_ref, wr_ref, cot_ref,
    y_ref, dx2_ref, gwo_ref, gwe_ref, gwr_ref, late_ref, datt_ref,
    ct_ref, cb_ref, x2_ref, h2_ref, acc_ref, dh2_ref, hid_ref, dpre_ref,
):
    rows = images * tokens
    row = lambda r: prm_ref[r : r + 1, :]
    to_tokens(images, tokens, lambda b, t: cot_ref[b, :, lane(t)].astype(f32), ct_ref)
    for tile in range(4):
        cb_ref[:, lane(tile)] = ct_ref[tile].astype(bf16)
    step = 80
    gain, shift = row(ROW_LATE_GAIN), row(ROW_LATE_SHIFT)
    x2_ref[...] = x1_ref[...] + dot(att_ref[...], wo_ref[...]) + row(ROW_OUT_BIAS)

    def norm(k, carry):
        at = pl.ds(pl.multiple_of(k * step, step), step)
        unit, _ = normalise(x2_ref[at, :], gain, shift)
        h2_ref[at, :] = (unit * gain + shift).astype(bf16)
        return carry

    lax.fori_loop(0, rows // step, norm, 0)
    acc_ref[...] = jnp.zeros_like(acc_ref)
    dh2_ref[...] = jnp.zeros_like(dh2_ref)
    half = rows // 2
    cw = we_ref.shape[2]

    def chunk(c, carry):
        bias = eb_ref[c]
        folded = jnp.zeros((8, cw), f32)
        for k in range(2):
            at = slice(k * half, (k + 1) * half)
            pre = dot(h2_ref[at, :], we_ref[c]) + bias
            dh = dot(cb_ref[at, :], wr_ref[c], 1, 1)
            gauss = jnp.exp(pre * pre * -0.5)
            t = 1.0 / (1.0 + (0.3275911 * 0.7071067811865476) * jnp.abs(pre))
            poly = t * (0.127414796 + t * (-0.142248368 + t * (0.7107068705 + t * (-0.7265760135 + t * 0.5307027145))))
            tail = poly * gauss
            cdf = jnp.where(pre >= 0, 1.0 - tail, tail)
            hid_ref[at, :] = (pre * cdf).astype(bf16)
            dpre = ((cdf + pre * gauss * 0.3989422804014327) * dh).astype(bf16)
            dpre_ref[at, :] = dpre
            folded = folded + fold_rows(dpre.astype(f32))
        late_ref[c + LATE_EXPAND_BIAS, :, 0:cw] = folded
        acc_ref[...] += dot(hid_ref[...], wr_ref[c])
        gwr_ref[c] = dot(hid_ref[...], cb_ref[...], 0, 0).astype(bf16)
        gwe_ref[c] = dot(h2_ref[...], dpre_ref[...], 0, 0).astype(bf16)
        dh2_ref[...] += dot(dpre_ref[...], we_ref[c], 1, 1)
        return carry

    lax.fori_loop(0, chunks, chunk, 0)

    def finish(k, carry):
        at = pl.ds(pl.multiple_of(k * step, step), step)
        x2 = x2_ref[at, :]
        out = x2 + acc_ref[at, :] + row(ROW_REDUCE_BIAS)
        unit, scale = normalise(x2, gain, shift)
        grad = dh2_ref[at, :]
        dy = cb_ref[at, :].astype(f32)
        dx2 = dy + normalise_back(grad, gain, unit, scale)
        dx2_ref[at, :] = dx2
        low = dx2.astype(bf16)
        dh2_ref[at, :] = low.astype(f32)
        for tile in range(4):
            ct_ref[tile, at, :] = out[:, lane(tile)]
        late = carry
        return (
            late[0] + fold_rows(grad * unit),
            late[1] + fold_rows(grad),
            late[2] + fold_rows(low.astype(f32)),
            late[3] + fold_rows(dy),
        )

    zero = jnp.zeros((8, 4 * LANES), f32)
    sums = lax.fori_loop(0, rows // step, finish, (zero,) * 4)
    for r, total in enumerate(sums):
        late_ref[r] = total
    for b in range(images):
        for tile in range(4):
            y_ref[b, :, lane(tile)] = ct_ref[tile, pl.ds(b, tokens, stride=images), :].astype(bf16)
    branch = dh2_ref[...].astype(bf16)
    gwo_ref[...] = dot(att_ref[...], branch, 0, 0).astype(bf16)
    datt_ref[...] = dot(branch, wo_ref[...], 1, 1).astype(bf16)


def attention_backward(
    images, tokens, datt_ref, dx2_ref, x1_ref, h1_ref, xt_ref, q_ref, v_ref, ks_ref, conv_ref,
    qi_ref, ki_ref, vi_ref, ctx_ref, prm_ref, wj_ref,
    gwj_ref, small_ref, dx_ref,
    da_ref, dai_ref, dc_ref, dq_ref, dk_ref, dv_ref, raw_ref, dx1_ref,
):
    rows = images * tokens
    width = 4 * LANES
    prm = lambda r, tile: prm_ref[r : r + 1, lane(tile)]
    small_ref[...] = jnp.zeros_like(small_ref)
    for tile in range(4):
        da_ref[tile] = datt_ref[:, lane(tile)].astype(f32)

    def image(b, carry):
        dai_ref[b, 48:PAD_TOK, :] = jnp.zeros((PAD_TOK - 48, width), bf16)
        for tile in range(4):
            dai_ref[b, 0:tokens, lane(tile)] = da_ref[tile, pl.ds(b, tokens, stride=images), :].astype(bf16)
        for g in range(2):
            at = slice(g * GROUP, (g + 1) * GROUP)
            grad = dai_ref[b, :, at]
            ctx = spread_context(ctx_ref[b, :, at])
            dctx = spread_context(compact_context(dot(qi_ref[b, :, at], grad, 0, 0) * SCALE))
            dq = dot(grad, ctx, 1, 1) * SCALE
            dk = dot(vi_ref[b, :, at], dctx, 1, 1)
            dv = dot(ki_ref[b, :, at], dctx)
            for t in range(2):
                here = pl.ds(b, tokens, stride=images)
                dq_ref[2 * g + t, here, :] = dq[0:tokens, lane(t)]
                dk_ref[2 * g + t, here, :] = dk[0:tokens, lane(t)]
                dv_ref[2 * g + t, here, :] = dv[0:tokens, lane(t)]
        return carry

    lax.fori_loop(0, images, image, 0)

    def relative(tile, extent):
        at = lambda n: slice(n * images, (n + 1) * images)
        bias_q = jnp.zeros((images, LANES), f32)
        bias_all = jnp.zeros((images, LANES), f32)
        dot_sum = jnp.zeros((images, LANES), f32)
        for n in range(tokens):
            grad = da_ref[tile, at(n), :]
            dq = (dq_ref[tile, at(n), :] + grad * conv_ref[tile, at(n), :]).astype(bf16)
            raw_ref[at(n), lane(tile)] = dq
            bias_q = bias_q + dq.astype(f32)
            dc = grad * q_ref[tile, at(n), :]
            dc_ref[tile, at(n), :] = dc
            if n > 0:
                bias_all = bias_all + dc
            dot_sum = dot_sum + dk_ref[tile, at(n), :] * ks_ref[tile, at(n), :]
        for n in range(tokens):
            soft = ks_ref[tile, at(n), :]
            raw_ref[at(n), lane(tile + 4)] = (soft * (dk_ref[tile, at(n), :] - dot_sum)).astype(bf16)
        small_ref[OUT_BIAS_Q, :, lane(tile)] = fold_rows(bias_q)
        small_ref[OUT_BIAS_ALL, :, lane(tile)] = fold_rows(bias_all)
        first = dv_ref[tile, at(0), :].astype(bf16)
        raw_ref[at(0), lane(tile + 8)] = first
        sums = [first.astype(f32)]

        def emit(i, total):
            for j in range(GRID):
                here = cell_rows(images, i * GRID + j)
                dv = (dv_ref[tile, here, :] + total[j]).astype(bf16)
                raw_ref[here, lane(tile + 8)] = dv
                sums[0] = sums[0] + dv.astype(f32)

        depthwise_rows(
            lambda r: grid_row(dc_ref, tile, images, r),
            lambda ab: prm(full_tap(extent, *ab), tile),
            extent, True, emit,
        )
        small_ref[OUT_BIAS_V, :, lane(tile)] = fold_rows(sums[0])
        extra = (GRID - extent) // 2

        def emit_tap(a, b, total):
            small_ref[OUT_KERNEL_ALL + (a + extra) * GRID + b + extra, :, lane(tile)] = fold_rows(total)

        kernel_grads(
            lambda i: grid_row(dc_ref, tile, images, i),
            lambda r: grid_row(v_ref, tile, images, r),
            extent, emit_tap,
        )

    tile_extents(relative)

    for part in range(3):
        at = slice(part * width, (part + 1) * width)
        gwj_ref[:, at] = dot(h1_ref[...], raw_ref[:, at], 0, 0).astype(bf16)
    dx1_ref[...] = dot(raw_ref[...], wj_ref[...], 1, 1)
    gain = prm_ref[ROW_EARLY_GAIN : ROW_EARLY_GAIN + 1, :]
    shift = prm_ref[ROW_EARLY_SHIFT : ROW_EARLY_SHIFT + 1, :]
    step = 80

    def back(k, carry):
        at = pl.ds(pl.multiple_of(k * step, step), step)
        grad = dx1_ref[at, :]
        unit, scale = normalise(x1_ref[at, :], gain, shift)
        total = dx2_ref[at, :] + normalise_back(grad, gain, unit, scale)
        for tile in range(4):
            da_ref[tile, at, :] = total[:, lane(tile)]
        return carry[0] + fold_rows(grad * unit), carry[1] + fold_rows(grad)

    zero = jnp.zeros((8, width), f32)
    sums = lax.fori_loop(0, rows // step, back, (zero, zero))
    small_ref[OUT_EARLY_GAIN] = sums[0]
    small_ref[OUT_EARLY_SHIFT] = sums[1]

    def position(tile, carry):
        bias = [jnp.zeros((images, LANES), f32)]
        dc_ref[tile, 0:images, :] = da_ref[tile, 0:images, :]

        def emit(i, total):
            own = grid_row(da_ref, tile, images, i)
            for j in range(GRID):
                dc_ref[tile, cell_rows(images, i * GRID + j), :] = own[j] + total[j]
                bias[0] = bias[0] + own[j]

        depthwise_rows(
            lambda r: grid_row(da_ref, tile, images, r),
            lambda ab: prm(ROW_POS_KERNEL + ab[0] * 3 + ab[1], tile),
            3, True, emit,
        )
        small_ref[OUT_POS_BIAS, :, lane(tile)] = fold_rows(bias[0])

        def emit_tap(a, b, total):
            small_ref[OUT_POS_KERNEL + a * 3 + b, :, lane(tile)] = fold_rows(total)

        kernel_grads(
            lambda i: grid_row(da_ref, tile, images, i),
            lambda r: grid_row(xt_ref, tile, images, r),
            3, emit_tap,
        )
        return carry

    lax.fori_loop(0, 4, position, 0)
    for b in range(images):
        for tile in range(4):
            dx_ref[b, :, lane(tile)] = dc_ref[tile, pl.ds(b, tokens, stride=images), :].astype(bf16)


def call(kernel, outs, scratch):
    return pl.pallas_call(
        kernel,
        out_shape=[jax.ShapeDtypeStruct(shape, dtype) for shape, dtype in outs],
        scratch_shapes=[pltpu.VMEM(shape, dtype) for shape, dtype in scratch],
        compiler_params=pltpu.CompilerParams(vmem_limit_bytes=VMEM_BYTES),
    )


def pack_params(position_kernel, position_bias, early_gain, early_shift, joint_bias, small_kernel, small_bias,
                middle_kernel, middle_bias, large_kernel, large_bias, output_bias, late_gain, late_shift, reduce_bias):
    width = position_bias.shape[0]
    kernel_all = jnp.concatenate(
        [
            jnp.pad(small_kernel, ((2, 2), (2, 2), (0, 0))),
            jnp.pad(middle_kernel, ((1, 1), (1, 1), (0, 0))),
            large_kernel,
        ],
        axis=2,
    ).reshape(CELLS, width)
    return jnp.concatenate(
        [
            position_bias[None], early_gain[None], early_shift[None], joint_bias.reshape(2, width),
            jnp.concatenate([small_bias, middle_bias, large_bias])[None],
            output_bias[None], late_gain[None], late_shift[None], reduce_bias[None],
            position_kernel.reshape(9, width), kernel_all,
            jnp.zeros((PARAM_ROWS - ROW_KERNEL_ALL - CELLS, width), bf16),
        ],
        axis=0,
    ).astype(f32)


def block(block_input, params, joint_weight, output_weight, expand_weight, expand_bias, reduce_weight, cotangent):
    images, tokens, width = block_input.shape
    rows = images * tokens
    chunks, _, cw = expand_weight.shape
    tiled = ((4, rows, LANES), f32)
    flat = ((rows, width), f32)
    low = ((rows, width), bf16)
    per_image = ((images, PAD_TOK, width), bf16)
    xt, x1, h1, q, v, ks, conv, qi, ki, vi, ctx, att = call(
        partial(attention_forward, images, tokens),
        [tiled, flat, low, tiled, tiled, tiled, tiled, per_image, per_image, per_image,
         ((images, HEAD, width), bf16), low],
        [tiled],
    )(block_input, params, joint_weight)
    y, dx2, gwo, gwe, gwr, late, datt = call(
        partial(feed_forward, images, tokens, chunks),
        [((images, tokens, width), bf16), flat, ((width, width), bf16), ((chunks, width, cw), bf16),
         ((chunks, cw, width), bf16), ((LATE_EXPAND_BIAS + chunks, 8, width), f32), low],
        [tiled, low, flat, low, flat, flat, ((rows, cw), bf16), ((rows, cw), bf16)],
    )(att, x1, params, expand_bias, output_weight, expand_weight, reduce_weight, cotangent)
    gwj, small, dx = call(
        partial(attention_backward, images, tokens),
        [((width, 3 * width), bf16), ((SMALL_ROWS, 8, width), f32), ((images, tokens, width), bf16)],
        [tiled, per_image, tiled, tiled, tiled, tiled, ((rows, 3 * width), bf16), flat],
    )(datt, dx2, x1, h1, xt, q, v, ks, conv, qi, ki, vi, ctx, params, joint_weight)
    return y, dx, gwj, gwo, gwe, gwr, jnp.sum(small, axis=1), jnp.sum(late, axis=1)


def per_device(
    block_input, position_kernel, position_bias, early_gain, early_shift, joint_weight, joint_bias,
    small_kernel, small_bias, middle_kernel, middle_bias, large_kernel, large_bias,
    output_weight, output_bias, late_gain, late_shift, expand_weight, expand_bias,
    reduce_weight, reduce_bias, cotangent,
):
    width = block_input.shape[2]
    parts = lax.axis_size("tensor")
    params = pack_params(
        position_kernel, position_bias, early_gain, early_shift, joint_bias, small_kernel, small_bias,
        middle_kernel, middle_bias, large_kernel, large_bias, output_bias, late_gain, late_shift, reduce_bias,
    )
    whole_out = lax.all_gather(output_weight, "tensor", axis=0, tiled=True)
    whole_expand = lax.all_gather(expand_weight, "tensor")
    whole_bias = lax.all_gather(expand_bias, "tensor").astype(f32)[:, None, :]
    whole_reduce = lax.all_gather(reduce_weight, "tensor")
    y, dx, gwj, gwo, gwe, gwr, small, late = block(
        block_input, params, joint_weight, whole_out, whole_expand, whole_bias, whole_reduce, cotangent
    )
    gwo, gwe, gwr = (
        lax.psum(lax.psum_scatter(part, "tensor", scatter_dimension=0, tiled=True), "dp").astype(f32)
        for part in (gwo, gwe.reshape(-1, gwe.shape[2]), gwr.reshape(-1, width))
    )
    gwj, small, late = lax.psum((gwj.astype(f32), small, late), ("dp", "tensor"))
    g_bias = lax.dynamic_slice_in_dim(late, LATE_EXPAND_BIAS + lax.axis_index("tensor"), 1, 0)
    g_bias = g_bias[0, : expand_bias.shape[0]]
    return unpack(y, dx, gwj, gwo, gwe, gwr, small, late, g_bias, small_kernel, middle_kernel)


def unpack(y, dx, gwj, gwo, gwe, gwr, small, late, g_bias, small_kernel, middle_kernel):
    width = small.shape[1]
    kernel_all = small[OUT_KERNEL_ALL : OUT_KERNEL_ALL + CELLS].reshape(GRID, GRID, width)
    bias_all = small[OUT_BIAS_ALL]
    one = small_kernel.shape[2]
    two = one + middle_kernel.shape[2]
    return (
        y, dx, small[OUT_POS_KERNEL : OUT_POS_KERNEL + 9].reshape(3, 3, width),
        small[OUT_POS_BIAS], small[OUT_EARLY_GAIN], small[OUT_EARLY_SHIFT], gwj,
        small[OUT_BIAS_Q : OUT_BIAS_V + 1].reshape(-1),
        kernel_all[2:5, 2:5, :one], bias_all[:one], kernel_all[1:6, 1:6, one:two], bias_all[one:two],
        kernel_all[:, :, two:], bias_all[two:],
        gwo, late[LATE_OUT_BIAS], late[LATE_GAIN], late[LATE_SHIFT], gwe, g_bias, gwr, late[LATE_REDUCE_BIAS],
    )


def solution(mesh):
    images = P(("dp", "tensor"), None, None)
    in_specs = (images,) + (P(),) * 12 + (
        P("tensor", None), P(), P(), P(), P(None, "tensor"), P("tensor"), P("tensor", None), P(), images,
    )
    out_specs = (images, images) + (P(),) * 12 + (
        P("tensor", None), P(), P(), P(), P(None, "tensor"), P("tensor"), P("tensor", None), P(),
    )
    return jax.shard_map(per_device, mesh=mesh, in_specs=in_specs, out_specs=out_specs, check_vma=False)
```

time: 703 us -> 479 us (0.68)
  other arithmetic: 122 us -> 9.13 us
  Pallas kernels: 0 us -> 88 us
  waiting for transfers between devices: 315 us -> 227 us
  matrix products: 83.2 us -> 0 us
  local copies, waits for them, and re-layouts: 104 us -> 22.4 us
  blocking collectives: 54.2 us -> 117 us
    psum x3 -> x2, waiting for transfers between devices: 301 us -> 90.6 us  [the longest x1 56.3 us: per_device(): lax.psum(lax.psum_scatter(part, 'tensor', scatter_dimension=0, tiled=True...]
    reduce_scatter x3, waiting for transfers between devices: 12.5 us -> 107 us  [per_device(): lax.psum_scatter(part, 'tensor', scatter_dimension=0, tiled=True)]
    pallas_call x0 -> x3, Pallas kernels: none -> 88 us  [the longest x1 32.6 us: block(): call(partial(attention_backward, images, tokens), [((width, 3 * width), b...]
    dot_general x18 -> x0, matrix products: 83.2 us -> none  [the longest x1 19.9 us: per_device(): jnp.dot(normed_group, expand_weight, preferred_element_type=f32)]
    psum x1, blocking collectives: 12.2 us -> 82.7 us  [per_device(): lax.psum((gwj.astype(f32), small, late), ('dp', 'tensor'))]
    reduce_sum x16 -> x2, other arithmetic: 35 us -> 2.18 us  [the longest x1 2.14 us: block(): jnp.sum(small, axis=1)]
    add_any x5 -> x0, other arithmetic: 30.4 us -> none  [the longest x3 29.6 us: depthwise(): padded[:, row_tap:row_tap + side_len, col_tap:col_tap + side_len, :]]
    unnamed x327 -> x27, local copies, waits for them, and re-layouts: 35.6 us -> 6.94 us
  transfers between devices with their start and end apart: 8 -> 7, of which waited for: 4 -> 6; matrix products, arithmetic and copies ran while one was open for 32% -> 5% of each run, Pallas kernels for 0% -> 6%
where the time goes in v2:
time: 479 us
  waiting for transfers between devices  227 us (47%)
  blocking collectives  117 us (24%)
  Pallas kernels  88 us (18%)
  local copies, waits for them, and re-layouts  22.4 us (5%)
  between operations  14.3 us (3%)
  other arithmetic  9.13 us (2%)
    reduce_scatter x3, waiting for transfers between devices, per_device(): lax.psum_scatter(part, 'tensor', scatter_dimension=0, tiled=True)  107 us
    psum x1, blocking collectives, per_device(): lax.psum((gwj.astype(f32), small, late), ('dp', 'tensor'))  82.7 us
    psum x1, waiting for transfers between devices, per_device(): lax.psum(lax.psum_scatter(part, 'tensor', scatter_dimension=0, tiled=True...  56.3 us
    psum x1, waiting for transfers between devices, per_device(): lax.psum((gwj.astype(f32), small, late), ('dp', 'tensor'))  34.3 us
    pallas_call x1, Pallas kernels, block(): call(partial(attention_backward, images, tokens), [((width, 3 * width), b...  32.6 us
    pallas_call x1, Pallas kernels, block(): call(partial(feed_forward, images, tokens, chunks), [((images, tokens, wi...  28.9 us
    all_gather x1, waiting for transfers between devices, per_device(): whole_reduce = lax.all_gather(reduce_weight, 'tensor')  26.6 us
    pallas_call x1, Pallas kernels, block(): call(partial(attention_forward, images, tokens), [tiled, flat, low, tiled...  26.5 us
  transfers between devices with their start and end apart: 7, of which 6 were waited for; matrix products, arithmetic and copies ran while one was open for 5% of the time, Pallas kernels for 6%

profile of v2, /device:TPU:0, one launch (start us, length us, event | category | flops | bytes accessed | tf_op | source)
XLA Modules:
  0.0 478.6 jit_solution(2058796811332745742)
XLA Ops:
  7.3 0.7 all-gather.7.cloned.1.call-update
  8.0 0.7 all-gather.9.cloned.1.call-update
  8.7 0.9 fusion.4
  9.6 0.7 reshape.72
  10.4 0.8 pad_maximum_fusion
  11.2 0.7 broadcast_in_dim.32
  11.8 0.7 broadcast_in_dim.33
  12.5 0.7 broadcast_in_dim.34
  13.2 0.7 broadcast_in_dim.36
  13.9 0.7 broadcast_in_dim.37
  14.6 0.7 broadcast_in_dim.38
  15.2 0.7 broadcast_in_dim.39
  15.9 0.7 reshape.71
  17.0 0.7 convert_element_type.20.prm_ref
  17.7 1.4 copy.48.x_ref
  19.1 1.4 copy.49.cot_ref
  20.5 13.8 %all-gather.3 = bf16[4,1,512]{2,1,0:T(2,128)(2,1)S(1)} all-gather(bf16[1,1,512]{2,1,0:T(2,128)(2,1)S(1)} %reshape.85), channel_id=2, replica_groups=mesh['dp'=8,'tensor'=4] {'tensor'}, dimensions={0}, use_global_device_ids=true | all-gather | bytes 5120 | tf_op jit(solution)/shard_map/all_gather | solution.py:561
  34.3 0.6 broadcast_in_dim.45.eb_ref
  34.9 26.5 %shard_map.381 = (f32[4,800,128]{2,1,0:T(8,128)}, f32[800,512]{1,0:T(8,128)}, bf16[800,512]{1,0:T(8,128)(2,1)}, f32[4,800,128]{2,1,0:T(8,128)}, f32[4,800,128]{2...) custom-call(bf16[16,50,512]{2,1,0:T(8,128)(2,1)} %copy.48.x_ref, ...), custom_call_target="tpu_custom_call" | custom-call | tf_op jit(solution)/shard_map/pallas_call | solution.py:527
  61.5 20.8 %all_gather.23.wo_ref = bf16[512,512]{1,0:T(8,128)(2,1)} all-gather(bf16[128,512]{1,0:T(8,128)(2,1)S(1)} %copy-done.6), channel_id=1, replica_groups=mesh['dp'=8,'tensor'=4] {'tensor'}, dimensions={0}, use_global_device_ids=true | all-gather | bytes 655360 | tf_op jit(solution)/shard_map/all_gather | solution.py:559
  82.3 26.6 %all-gather.9.cloned.1.call-done = bf16[2048,512]{1,0:T(8,128)(2,1)} async-done(((bf16[512,512]{1,0:T(8,128)(2,1)}), bf16[2048,512]{1,0:T(8,128)(2,1)}) %all-gather.9.cloned.1.call-update) | async-done | bytes 2097168 | tf_op jit(solution)/shard_map/all_gather | solution.py:562
  108.9 28.9 %shard_map.382 = (bf16[16,50,512]{2,1,0:T(8,128)(2,1)}, f32[800,512]{1,0:T(8,128)}, bf16[512,512]{1,0:T(8,128)(2,1)}, bf16[4,512,512]{2,1,0:T(8,128)(2,1)}, bf16...) custom-call(bf16[800,512]{1,0:T(8,128)(2,1)} %get-tuple-element.44.att_ref, ...), custom_call_target="tpu_custom_call" | custom-call | tf_op jit(solution)/shard_map/pallas_call | solution.py:533
  137.7 32.6 %shard_map.383 = (bf16[512,1536]{1,0:T(8,128)(2,1)}, f32[64,8,512]{2,1,0:T(8,128)}, bf16[16,50,512]{2,1,0:T(8,128)(2,1)}) custom-call(bf16[800,512]{1,0:T(8,128)(2,1)} %get-tuple-element.47.datt_ref, f32[800,512]{1,0:T(8,128)} %get-tuple-element.48.dx2_ref, f32[800,512]{1,0:T(8,128)} %get-tuple-element.45.x1_ref, bf16[800,512]{1,0:T(8,128)(2,1)} %get-tuple-element.49.h1_ref, ...), custom_call_target="tpu_custom_call" | custom-call | tf_op jit(solution)/shard_map/pallas_call | solution.py:539
  170.4 2.1 reduce_sum.18
  173.2 0.5 reduce-scatter.6.cloned.1.call-update
  174.9 1.1 copy.51
  176.1 1.1 copy.50
  177.2 82.7 %all-reduce.11 = (f32[512,1536]{1,0:T(8,128)}, f32[8,512]{1,0:T(8,128)S(1)}) all-reduce(bf16[512,1536]{1,0:T(8,128)(2,1)S(1)} %copy-done, f32[8,512]{1,0:T(8,128)S(1)} %reduce_sum.19), channel_id=1, replica_groups=mesh['dp'=8,'tensor'=4] {'dp','tensor'}, use_global_device_ids=true, to_apply=%region_2.3 | all-reduce | flops 790528 | bytes 4751360 | tf_op jit(solution)/shard_map/psum | solution.py:570
  259.9 0.6 fusion.7
  260.5 34.3 %all-reduce.8.cloned.1.call-done = f32[64,512]{1,0:T(8,128)} async-done(((f32[64,512]{1,0:T(8,128)}), f32[64,512]{1,0:T(8,128)}) %all-reduce.8.cloned.1.call-update) | async-done | bytes 131088 | tf_op jit(solution)/shard_map/psum | solution.py:570
  294.7 0.9 slice.85
  295.7 0.7 slice.90
  296.4 0.6 slice.88
  297.0 0.6 slice.86
  297.6 0.8 slice.80
  298.4 0.6 reshape.74
  299.0 0.7 slice_bitcast_fusion
  299.7 0.6 copy.52
  300.3 17.3 %reduce-scatter.4.cloned.1.call-done = bf16[128,512]{1,0:T(8,128)(2,1)} async-done(((bf16[512,512]{1,0:T(8,128)(2,1)}), bf16[128,512]{1,0:T(8,128)(2,1)}) %reduce-scatter.4.cloned.1.call-update) | async-done | bytes 131088 | tf_op jit(solution)/shard_map/reduce_scatter | solution.py:567
  317.6 44.3 %reduce-scatter.6.cloned.1.call-done = bf16[512,512]{1,0:T(8,128)(2,1)} async-done(((bf16[2048,512]{1,0:T(8,128)(2,1)}), bf16[512,512]{1,0:T(8,128)(2,1)}) %reduce-scatter.6.cloned.1.call-update) | async-done | bytes 524304 | tf_op jit(solution)/shard_map/reduce_scatter | solution.py:567
  361.9 45.5 %reduce-scatter.8.cloned.1.call-done = bf16[512,512]{1,0:T(8,128)(2,1)} async-done(((bf16[2048,512]{1,0:T(8,128)(2,1)}), bf16[512,512]{1,0:T(8,128)(2,1)}) %reduce-scatter.8.cloned.1.call-update) | async-done | bytes 524304 | tf_op jit(solution)/shard_map/reduce_scatter | solution.py:567
  407.4 1.2 slice_bitcast_fusion.1
  408.6 1.4 fusion.5
  410.0 1.4 fusion.6
  411.4 56.3 %all-reduce.10.cloned.1.call-done = (bf16[128,512]{1,0:T(8,128)(2,1)}, bf16[512,512]{1,0:T(8,128)(2,1)}, bf16[512,512]{1,0:T(8,128)(2,1)}) async-done(((bf16[128,512]{1,0:T(8,128)(2,1)}, bf16[512,512]{1,0:T(8,128)(2,1)}, bf16[512,512]{1,0:T(8,128)(2,1)}), (bf16[128,512]{1,0:T(8,128)(2,1)}, bf16[512,512]{1,0:T(8,128)(2,1)}, bf16[512,512]{1,0:T(8,128)(2,1)})) %all-reduce.10.cloned.1.call-update) | async-done | bytes 1179664 | tf_op jit(solution)/shard_map/psum | solution.py:567
  467.7 2.2 convert_element_type.23
  469.9 1.1 convert_element_type.24
  471.0 0.7 convert_element_type.22
  (39 shorter events, 2.4 us)
Async XLA Ops:
  7.2 10.5 %copy-start.3 = (bf16[16,50,512]{2,0,1:T(8,128)(2,1)S(1)}, bf16[16,50,512]{2,0,1:T(8,128)(2,1)}, u32[]{:S(2)}) copy-start(bf16[16,50,512]{2,0,1:T(8,128)(2,1)} %param.22) | copy-start | bytes 2457604
  7.2 11.9 %copy-start.4 = (bf16[16,50,512]{2,0,1:T(8,128)(2,1)S(1)}, bf16[16,50,512]{2,0,1:T(8,128)(2,1)}, u32[]{:S(2)}) copy-start(bf16[16,50,512]{2,0,1:T(8,128)(2,1)} %param.43) | copy-start | bytes 2457604
  7.2 75.0 %all-gather.7.cloned.1.call-start = ((), (), s32[]{:S(2)}) async-start(), calls=%async_computation.7 | async-start | bytes 2621440 | tf_op jit(solution)/shard_map/all_gather | solution.py:560
  7.9 100.9 %all-gather.9.cloned.1.call-start = ((), (), s32[]{:S(2)}) async-start(), calls=%async_computation.8 | async-start | bytes 2621440 | tf_op jit(solution)/shard_map/all_gather | solution.py:562
  8.7 286.0 %all-reduce.8.cloned.1.call-start = ((), (), s32[]{:S(2)}) async-start(), calls=%async_computation.3 | async-start | bytes 262144 | tf_op jit(solution)/shard_map/psum | solution.py:570
  17.7 2.8 copy-start.9
  20.5 40.9 %copy-start.6 = (bf16[128,512]{1,0:T(8,128)(2,1)S(1)}, bf16[128,512]{1,0:T(8,128)(2,1)}, u32[]{:S(2)}) copy-start(bf16[128,512]{1,0:T(8,128)(2,1)} %param.35) | copy-start | bytes 393220
  172.6 145.1 %reduce-scatter.4.cloned.1.call-start = ((), (), s32[]{:S(2)}) async-start(), calls=%async_computation.4 | async-start | bytes 655360 | tf_op jit(solution)/shard_map/reduce_scatter | solution.py:567
  173.1 188.8 %reduce-scatter.6.cloned.1.call-start = ((), (), s32[]{:S(2)}) async-start(), calls=%async_computation.5 | async-start | bytes 2621440 | tf_op jit(solution)/shard_map/reduce_scatter | solution.py:567
  173.2 1.2 copy-start.8
  173.7 1.2 copy-start.2
  173.7 233.7 %reduce-scatter.8.cloned.1.call-start = ((), (), s32[]{:S(2)}) async-start(), calls=%async_computation.6 | async-start | bytes 2621440 | tf_op jit(solution)/shard_map/reduce_scatter | solution.py:567
  173.8 2.3 copy-start.1
  174.3 293.4 %all-reduce.10.cloned.1.call-start = ((), (), s32[]{:S(2)}) async-start(), calls=%async_computation.9 | async-start | bytes 2359296 | tf_op jit(solution)/shard_map/psum | solution.py:567
  174.9 2.3 copy-start
  467.7 2.2 copy-start.5
  467.7 3.3 copy-start.7
Sparse Core Ops, SparseCore 0:
  9.6 48.8 all-gather.6
  60.0 48.8 all-gather.8
  172.7 122.0 all-reduce.7
  296.9 20.6 reduce-scatter.3
  319.7 42.1 reduce-scatter.5
  364.2 43.1 reduce-scatter.7
  410.9 56.8 all-reduce.9

commit v3 on v2

v3 whole, which is shorter than its diff:
```python
import math
from functools import partial

import jax
import jax.numpy as jnp
from jax import lax
from jax.experimental import pallas as pl
from jax.experimental.pallas import tpu as pltpu
from jax.sharding import PartitionSpec as P

HEADS = 8
HEAD = 64
GRID = 7
CELLS = GRID * GRID
NORM_EPS = 1e-06
SCALE = HEAD**-0.5
LANES = 128
GROUP = 256
PAD_TOK = 64
VMEM_BYTES = 62 * 1024 * 1024

f32 = jnp.float32
bf16 = jnp.bfloat16

ROW_POS_BIAS, ROW_EARLY_GAIN, ROW_EARLY_SHIFT, ROW_BIAS_Q, ROW_BIAS_V = 0, 1, 2, 3, 4
ROW_BIAS_ALL, ROW_OUT_BIAS, ROW_LATE_GAIN, ROW_LATE_SHIFT, ROW_REDUCE_BIAS = 5, 6, 7, 8, 9
ROW_POS_KERNEL, ROW_KERNEL_ALL = 10, 19
PARAM_ROWS = 72

OUT_POS_KERNEL, OUT_KERNEL_ALL = 0, 9
OUT_POS_BIAS, OUT_EARLY_GAIN, OUT_EARLY_SHIFT, OUT_BIAS_Q, OUT_BIAS_V, OUT_BIAS_ALL = 58, 59, 60, 61, 62, 63
OUT_LATE_GAIN, OUT_LATE_SHIFT, OUT_OUT_BIAS, OUT_REDUCE_BIAS, OUT_EXPAND_BIAS = 64, 65, 66, 67, 68
MESH = pl.DeviceIdType.MESH


def lane(tile):
    if isinstance(tile, int):
        return slice(tile * LANES, (tile + 1) * LANES)
    return pl.ds(pl.multiple_of(tile * LANES, LANES), LANES)


def taps(extent):
    return range(extent)


def columns(shift):
    return range(max(0, -shift), min(GRID, GRID - shift))


def depthwise_rows(get_row, get_weight, extent, flip, emit):
    margin = extent // 2
    for i in range(GRID):
        total = [None] * GRID
        for a in range(extent):
            r = i + a - margin
            if not 0 <= r < GRID:
                continue
            row = get_row(r)
            for b in range(extent):
                weight = get_weight((extent - 1 - a, extent - 1 - b) if flip else (a, b))
                for j in columns(b - margin):
                    term = row[j + b - margin] * weight
                    total[j] = term if total[j] is None else total[j] + term
        emit(i, total)


def kernel_grads(get_left, get_right, extent, emit):
    margin = extent // 2
    for a in range(extent):
        total = [None] * extent
        for i in range(GRID):
            r = i + a - margin
            if not 0 <= r < GRID:
                continue
            left, right = get_left(i), get_right(r)
            for b in range(extent):
                for j in columns(b - margin):
                    term = left[j] * right[j + b - margin]
                    total[b] = term if total[b] is None else total[b] + term
        for b in range(extent):
            emit(a, b, total[b])


def cell_rows(images, cell, count=1):
    return slice((1 + cell) * images, (1 + cell + count) * images)


def grid_row(ref, tile, images, i):
    block = ref[tile, cell_rows(images, i * GRID, GRID), :]
    return [block[j * images : (j + 1) * images] for j in range(GRID)]


def full_tap(extent, a, b):
    extra = (GRID - extent) // 2
    return ROW_KERNEL_ALL + (a + extra) * GRID + b + extra


def tile_extents(body):
    body(0, 3)
    body(1, 5)

    def rest(tile, carry):
        body(tile, 7)
        return carry

    lax.fori_loop(2, 4, rest, 0)


def normalise(block):
    centre = jnp.mean(block, axis=-1, keepdims=True)
    centred = block - centre
    spread = jnp.mean(centred * centred, axis=-1, keepdims=True)
    scale = lax.rsqrt(spread + NORM_EPS)
    return centred * scale, scale


def normalise_back(grad, gain, unit, scale):
    scaled = grad * gain
    mean_one = jnp.mean(scaled, axis=-1, keepdims=True)
    mean_two = jnp.mean(scaled * unit, axis=-1, keepdims=True)
    return (scaled - mean_one - unit * mean_two) * scale


def fold_rows(block):
    return jnp.sum(block.reshape(block.shape[0] // 8, 8, block.shape[1]), axis=0)


def dot(left, right, left_dim=1, right_dim=0):
    return lax.dot_general(
        left, right, (((left_dim,), (right_dim,)), ((), ())), preferred_element_type=f32
    )


def head_of(rows, columns_):
    return lax.broadcasted_iota(jnp.int32, (rows, columns_), 1) // HEAD


def compact_context(full):
    heads = head_of(HEAD, GROUP)
    total = jnp.zeros((HEAD, GROUP), f32)
    for h in range(GROUP // HEAD):
        total = jnp.where(heads == h, full[h * HEAD : (h + 1) * HEAD, :], total)
    return total.astype(bf16)


def spread_context(compact):
    heads = head_of(HEAD, GROUP)
    wide = compact.astype(f32)
    return jnp.concatenate(
        [jnp.where(heads == h, wide, 0.0).astype(bf16) for h in range(GROUP // HEAD)], axis=0
    )


def padded(count, unit):
    return -(-count // unit) * unit


class Ring:
    def __init__(self, pairs, depth, send_sems, recv_sems):
        self.dp = lax.axis_index("dp")
        self.me = lax.axis_index("tensor")
        self.planes, self.depth = pairs, depth
        group = 2 * pairs
        self.base = lax.div(self.dp, group) * group
        self.core = lax.rem(self.dp, 2)
        self.spot = lax.div(lax.rem(self.dp, group), 2)
        self.send_sems, self.recv_sems, self.used = send_sems, recv_sems, 0
        self.sent = []

    def twin(self):
        return {"dp": self.base + self.spot * 2 + (1 - self.core), "tensor": self.me}

    def plane(self, k):
        return {"dp": self.base + lax.rem(self.spot + k, self.planes) * 2 + self.core, "tensor": self.me}

    def plane_spot(self, k):
        return lax.rem(self.spot + k, self.planes)

    def stack(self, k):
        return {"dp": self.dp, "tensor": lax.rem(self.me + k, self.depth)}

    def everyone(self):
        return (
            [self.twin()]
            + [self.plane(k) for k in range(1, self.planes)]
            + [self.stack(k) for k in range(1, self.depth)]
        )

    def piece(self, rows, spot, core=None):
        each = rows // (2 * self.planes)
        core = self.core if core is None else core
        return pl.ds(pl.multiple_of((core * self.planes + spot) * each, each), each)

    def half(self, rows, core):
        return pl.ds(pl.multiple_of(core * (rows // 2), rows // 2), rows // 2)

    def send(self, source, target, device):
        at = self.used
        self.used += 1
        copy = pltpu.make_async_remote_copy(
            src_ref=source, dst_ref=target, send_sem=self.send_sems.at[at], recv_sem=self.recv_sems.at[at],
            device_id=device, device_id_type=MESH,
        )
        copy.start()
        self.sent.append(copy)
        return copy


def arrive(copies):
    for copy in copies:
        copy.wait_recv()


class Reduction:
    def __init__(self, ring, grads, twin_box, plane_box, stack_box, out, whole, relative):
        self.ring, self.grads, self.out, self.whole, self.relative = ring, grads, out, whole, relative
        self.twin_box, self.plane_box, self.stack_box = twin_box, plane_box, stack_box
        self.rows = grads.shape[1]
        self.depth = grads.shape[0]
        self.pairs, self.planes = {}, {}
        self.all = slice(0, self.depth)

    def slot(self, k):
        return k if self.relative else lax.rem(self.ring.me + k, self.depth)

    def pair(self, part):
        ring = self.ring
        away = ring.half(self.rows, 1 - ring.core)
        self.pairs[str(part)] = ring.send(self.grads.at[part, away], self.twin_box.at[part], ring.twin())

    def plane(self, part):
        ring = self.ring
        arrive([self.pairs[str(part)]])
        mine = ring.half(self.rows, ring.core)
        self.grads[part, mine] = (
            self.grads[part, mine].astype(f32) + self.twin_box[part].astype(f32)
        ).astype(bf16)
        self.planes[str(part)] = [
            ring.send(
                self.grads.at[part, ring.piece(self.rows, ring.plane_spot(k))],
                self.plane_box.at[k - 1, part], ring.plane(k),
            )
            for k in range(1, ring.planes)
        ]

    def gather_plane(self, part):
        ring = self.ring
        arrive(self.planes[str(part)])
        mine = ring.piece(self.rows, ring.spot)
        total = self.grads[part, mine].astype(f32)
        for k in range(1, ring.planes):
            total = total + self.plane_box[k - 1, part].astype(f32)
        self.grads[part, mine] = total.astype(bf16)

    def stack(self):
        ring = self.ring
        mine = ring.piece(self.rows, ring.spot)
        self.stacks = [
            ring.send(self.grads.at[self.slot(k), mine], self.stack_box.at[k - 1], ring.stack(k))
            for k in range(1, self.depth)
        ]

    def settle(self):
        ring = self.ring
        arrive(self.stacks)
        mine = ring.piece(self.rows, ring.spot)
        total = self.grads[self.slot(0), mine].astype(f32)
        for k in range(1, self.depth):
            total = total + self.stack_box[k - 1].astype(f32)
        done = total.astype(bf16)
        if self.whole:
            self.out[ring.me, mine] = done
            place = self.out.at[ring.me, mine]
            self.spread = [ring.send(place, place, ring.stack(k)) for k in range(1, self.depth)]
        else:
            self.out[mine] = done
            self.to_plane()

    def to_plane(self):
        ring = self.ring
        mine = ring.piece(self.rows, ring.spot)
        if self.whole:
            arrive(self.spread)
            place = self.out.at[:, mine]
        else:
            place = self.out.at[mine]
        self.back = [ring.send(place, place, ring.plane(k)) for k in range(1, ring.planes)]

    def to_twin(self):
        ring = self.ring
        arrive(self.back)
        mine = ring.half(self.rows, ring.core)
        place = self.out.at[:, mine] if self.whole else self.out.at[mine]
        self.last = ring.send(place, place, ring.twin())

    def finish(self):
        arrive([self.last])


class Gather:
    def __init__(self, ring, shard, box, relative):
        self.ring, self.box, self.relative = ring, box, relative
        self.depth, self.rows = box.shape[0], box.shape[1]
        mine = ring.piece(self.rows, ring.spot)
        self.first = [
            ring.send(
                shard.at[mine], box.at[(self.depth - k) if relative else ring.me, mine], ring.stack(k)
            )
            for k in range(1, self.depth)
        ]

    def places(self, rows):
        if self.relative:
            return [self.box.at[1 : self.depth, rows]]
        return [self.box.at[lax.rem(self.ring.me + k, self.depth), rows] for k in range(1, self.depth)]

    def plane(self):
        ring = self.ring
        arrive(self.first)
        mine = ring.piece(self.rows, ring.spot)
        self.second = [
            ring.send(place, place, ring.plane(k))
            for k in range(1, ring.planes) for place in self.places(mine)
        ]

    def pair(self):
        ring = self.ring
        arrive(self.second)
        self.third = [
            ring.send(place, place, ring.twin()) for place in self.places(ring.half(self.rows, ring.core))
        ]

    def finish(self):
        arrive(self.third)


def wide(ref, at):
    return jnp.concatenate([ref[tile, at, :] for tile in range(4)], axis=1)


def put_wide(ref, at, block):
    for tile in range(4):
        ref[tile, at, :] = block[:, lane(tile)]


def whole_block(
    images, tokens, planes, depth,
    x_ref, cot_ref, prm_ref, wj_ref, wo_shard, we_shard, wr_shard, eb_shard,
    y_ref, dx_ref, gwo_ref, gwe_ref, gwr_ref, gwj_ref, gsm_ref,
    x1_ref, x2_ref, q_ref, v_ref, ks_ref, conv_ref, fac_ref, dc_ref, one_ref, two_ref, three_ref,
    h1_ref, att_ref, h2_ref, raw_ref,
    qi_ref, ki_ref, vi_ref, dai_ref, ctx_ref, sums_ref,
    wo_ref, we_ref, wr_ref, eb_ref,
    go_ref, ge_ref, gr_ref, gj_ref, gs_ref,
    to_ref, te_ref, tr_ref, tj_ref, ts_ref,
    po_ref, pe_ref, pr_ref, pj_ref, ps_ref,
    so_ref, se_ref, sr_ref, sj_ref, ss_ref,
    send_sems, recv_sems, local_sems,
):
    ring = Ring(planes, depth, send_sems, recv_sems)
    barrier = pltpu.get_barrier_semaphore()
    for device in ring.everyone():
        pl.semaphore_signal(barrier, inc=1, device_id=device, device_id_type=MESH)
    pl.semaphore_wait(barrier, planes + depth - 1)

    rows = images * tokens
    width = 4 * LANES
    step = 5 * images
    steps = rows // step
    share = width // depth
    cw = we_ref.shape[2]
    prm = lambda row, tile: prm_ref[row : row + 1, lane(tile)]
    row = lambda r: prm_ref[r : r + 1, :]
    block_at = lambda k: pl.ds(pl.multiple_of(k * step, step), step)

    get_out = Gather(ring, wo_shard, wo_ref, False)
    get_expand = Gather(ring, we_shard, we_ref, True)
    get_reduce = Gather(ring, wr_shard, wr_ref, True)
    gathers = (get_out, get_expand, get_reduce)
    get_bias = [ring.send(eb_shard, eb_ref.at[depth - k], ring.stack(k)) for k in range(1, depth)]
    own = [
        pltpu.make_async_copy(source, target, local_sems.at[at])
        for at, (source, target) in enumerate(
            ((wo_shard, wo_ref.at[ring.me]), (we_shard, we_ref.at[0]), (wr_shard, wr_ref.at[0]), (eb_shard, eb_ref.at[0]))
        )
    ]
    for copy in own:
        copy.start()

    x_row = lambda tile, i: [
        x_ref[cell_rows(images, i * GRID + j), lane(tile)].astype(f32) for j in range(GRID)
    ]

    def position(tile, carry):
        x1_ref[tile, 0:images, :] = x_ref[0:images, lane(tile)].astype(f32)
        bias = prm(ROW_POS_BIAS, tile)

        def emit(i, total):
            here = x_row(tile, i)
            for j in range(GRID):
                x1_ref[tile, cell_rows(images, i * GRID + j), :] = here[j] + total[j] + bias

        depthwise_rows(
            partial(x_row, tile), lambda ab: prm(ROW_POS_KERNEL + ab[0] * 3 + ab[1], tile), 3, False, emit
        )
        return carry

    lax.fori_loop(0, 4, position, 0)

    def norm_of(source, target, gain, shift):
        def norm(k, carry):
            at = block_at(k)
            unit, _ = normalise(wide(source, at))
            target[at, :] = (unit * gain + shift).astype(bf16)
            return carry

        lax.fori_loop(0, steps, norm, 0)

    gain_one, shift_one = row(ROW_EARLY_GAIN), row(ROW_EARLY_SHIFT)
    norm_of(x1_ref, h1_ref, gain_one, shift_one)
    every = slice(0, rows)
    put_wide(v_ref, every, (dot(h1_ref[...], wj_ref[:, 2 * width :]) + row(ROW_BIAS_V)).astype(bf16).astype(f32))
    for gather in gathers:
        gather.plane()
    put_wide(ks_ref, every, dot(h1_ref[...], wj_ref[:, width : 2 * width]).astype(bf16).astype(f32))
    put_wide(q_ref, every, (dot(h1_ref[...], wj_ref[:, :width]) + row(ROW_BIAS_Q)).astype(bf16).astype(f32))

    token = lambda n: slice(n * images, (n + 1) * images)

    def soften(tile, carry):
        top = ks_ref[tile, token(0), :]
        for n in range(1, tokens):
            top = jnp.maximum(top, ks_ref[tile, token(n), :])
        total = jnp.zeros_like(top)
        for n in range(tokens):
            e = jnp.exp(ks_ref[tile, token(n), :] - top)
            ks_ref[tile, token(n), :] = e
            total = total + e
        scale = 1.0 / total
        for n in range(tokens):
            ks_ref[tile, token(n), :] = ks_ref[tile, token(n), :] * scale
        return carry

    lax.fori_loop(0, 4, soften, 0)

    def convolve(tile, extent):
        conv_ref[tile, 0:images, :] = jnp.zeros((images, LANES), f32)
        bias = prm(ROW_BIAS_ALL, tile)

        def emit(i, total):
            for j in range(GRID):
                conv_ref[tile, cell_rows(images, i * GRID + j), :] = total[j] + bias

        depthwise_rows(
            partial(grid_row, v_ref, tile, images), lambda ab: prm(full_tap(extent, *ab), tile),
            extent, False, emit,
        )

    tile_extents(convolve)
    for gather in gathers:
        gather.pair()

    def image(b, carry):
        for source, target in ((q_ref, qi_ref), (ks_ref, ki_ref), (v_ref, vi_ref)):
            target[b, 48:PAD_TOK, :] = jnp.zeros((PAD_TOK - 48, width), bf16)
            for tile in range(4):
                target[b, 0:tokens, lane(tile)] = source[tile, pl.ds(b, tokens, stride=images), :].astype(bf16)
        for g in range(2):
            at = slice(g * GROUP, (g + 1) * GROUP)
            compact = compact_context(dot(ki_ref[b, :, at], vi_ref[b, :, at], 0, 0))
            ctx_ref[b, :, at] = compact
            out = dot(qi_ref[b, :, at], spread_context(compact)) * SCALE
            for t in range(2):
                fac_ref[2 * g + t, pl.ds(b, tokens, stride=images), :] = out[0:tokens, lane(t)]
        return carry

    lax.fori_loop(0, images, image, 0)

    def combine(tile, carry):
        att_ref[:, lane(tile)] = (fac_ref[tile] + q_ref[tile] * conv_ref[tile]).astype(bf16)
        return carry

    lax.fori_loop(0, 4, combine, 0)

    for copy in own:
        copy.wait()
    arrive(get_bias)
    for gather in gathers:
        gather.finish()
    whole_out = jnp.concatenate([wo_ref[t, 0:share, :] for t in range(depth)], axis=0)
    branch = dot(att_ref[...], whole_out) + row(ROW_OUT_BIAS)
    for tile in range(4):
        x2_ref[tile] = x1_ref[tile] + branch[:, lane(tile)]
    gain_two, shift_two = row(ROW_LATE_GAIN), row(ROW_LATE_SHIFT)
    norm_of(x2_ref, h2_ref, gain_two, shift_two)

    send_expand = Reduction(ring, ge_ref, te_ref, pe_ref, se_ref, gwe_ref, False, True)
    send_reduce = Reduction(ring, gr_ref, tr_ref, pr_ref, sr_ref, gwr_ref, False, True)
    send_out = Reduction(ring, go_ref, to_ref, po_ref, so_ref, gwo_ref, False, False)
    send_joint = Reduction(ring, gj_ref, tj_ref, pj_ref, sj_ref, gwj_ref, True, False)
    send_small = Reduction(ring, gs_ref, ts_ref, ps_ref, ss_ref, gsm_ref, True, False)
    feed = (send_expand, send_reduce)
    acc_ref, dh2_ref = one_ref, two_ref
    hid_ref, dpre_ref = raw_ref.at[:, 0:cw], raw_ref.at[:, width : width + cw]
    datt_ref = raw_ref.at[:, 2 * width : 3 * width]
    half = rows // 2
    sums_ref[...] = jnp.zeros_like(sums_ref)
    for c in range(depth):
        bias = eb_ref[c, 0:1, :]
        folded = jnp.zeros((8, cw), f32)
        we, wr = we_ref[c], wr_ref[c, 0:cw, :]
        for k in range(2):
            at = slice(k * half, (k + 1) * half)
            pre = dot(h2_ref[at, :], we) + bias
            dh = dot(cot_ref[at, :], wr, 1, 1)
            gauss = jnp.exp(pre * pre * -0.5)
            t = 1.0 / (1.0 + (0.3275911 * 0.7071067811865476) * jnp.abs(pre))
            poly = t * (0.127414796 + t * (-0.142248368 + t * (0.7107068705 + t * (-0.7265760135 + t * 0.5307027145))))
            tail = poly * gauss
            cdf = jnp.where(pre >= 0, 1.0 - tail, tail)
            hid_ref[at, :] = (pre * cdf).astype(bf16)
            dpre = ((cdf + pre * gauss * 0.3989422804014327) * dh).astype(bf16)
            dpre_ref[at, :] = dpre
            folded = folded + fold_rows(dpre.astype(f32))
        sums_ref[OUT_EXPAND_BIAS + lax.rem(ring.me + c, depth), :, 0:cw] = folded
        ge_ref[c] = dot(h2_ref[...], dpre_ref[...], 0, 0).astype(bf16)
        gr_ref[c, 0:cw] = dot(hid_ref[...], cot_ref[...], 0, 0).astype(bf16)
        if gr_ref.shape[1] > cw:
            gr_ref[c, cw:] = jnp.zeros((gr_ref.shape[1] - cw, width), bf16)
        for part in feed:
            part.pair(c)
        out = dot(hid_ref[...], wr)
        back = dot(dpre_ref[...], we, 1, 1)
        for tile in range(4):
            if c == 0:
                acc_ref[tile] = out[:, lane(tile)]
                dh2_ref[tile] = back[:, lane(tile)]
            else:
                acc_ref[tile] += out[:, lane(tile)]
                dh2_ref[tile] += back[:, lane(tile)]
        if c >= 1:
            for part in feed:
                part.plane(c - 1)
        if c >= 2:
            for part in feed:
                part.gather_plane(c - 2)

    def finish(k, carry):
        at = block_at(k)
        x2 = wide(x2_ref, at)
        y_ref[at, :] = (x2 + wide(acc_ref, at) + row(ROW_REDUCE_BIAS)).astype(bf16)
        unit, scale = normalise(x2)
        grad = wide(dh2_ref, at)
        dy = cot_ref[at, :].astype(f32)
        dx2 = dy + normalise_back(grad, gain_two, unit, scale)
        put_wide(x2_ref, at, dx2)
        low = dx2.astype(bf16)
        datt_ref[at, :] = low
        return (
            carry[0] + fold_rows(grad * unit), carry[1] + fold_rows(grad),
            carry[2] + fold_rows(low.astype(f32)), carry[3] + fold_rows(dy),
        )

    zero = jnp.zeros((8, width), f32)
    sums = lax.fori_loop(0, steps, finish, (zero,) * 4)
    for r, total in zip((OUT_LATE_GAIN, OUT_LATE_SHIFT, OUT_OUT_BIAS, OUT_REDUCE_BIAS), sums):
        sums_ref[r] = total
    for part in feed:
        part.plane(depth - 1)
        if depth > 1:
            part.gather_plane(depth - 2)
    grad_out = dot(att_ref[...], datt_ref[...], 0, 0).astype(bf16)
    for t in range(depth):
        go_ref[t, 0:share, :] = grad_out[t * share : (t + 1) * share, :]
        if go_ref.shape[1] > share:
            go_ref[t, share:, :] = jnp.zeros((go_ref.shape[1] - share, width), bf16)
    send_out.pair(send_out.all)
    grad_att = dot(datt_ref[...], whole_out, 1, 1).astype(bf16).astype(f32)
    da_ref, dq_ref, dk_ref, dv_ref = fac_ref, one_ref, two_ref, three_ref
    put_wide(da_ref, every, grad_att)
    send_out.plane(send_out.all)

    def image_back(b, carry):
        dai_ref[b, 48:PAD_TOK, :] = jnp.zeros((PAD_TOK - 48, width), bf16)
        for tile in range(4):
            dai_ref[b, 0:tokens, lane(tile)] = da_ref[tile, pl.ds(b, tokens, stride=images), :].astype(bf16)
        for g in range(2):
            at = slice(g * GROUP, (g + 1) * GROUP)
            grad = dai_ref[b, :, at]
            ctx = spread_context(ctx_ref[b, :, at])
            dctx = spread_context(compact_context(dot(qi_ref[b, :, at], grad, 0, 0) * SCALE))
            dq = dot(grad, ctx, 1, 1) * SCALE
            dk = dot(vi_ref[b, :, at], dctx, 1, 1)
            dv = dot(ki_ref[b, :, at], dctx)
            for t in range(2):
                here = pl.ds(b, tokens, stride=images)
                dq_ref[2 * g + t, here, :] = dq[0:tokens, lane(t)]
                dk_ref[2 * g + t, here, :] = dk[0:tokens, lane(t)]
                dv_ref[2 * g + t, here, :] = dv[0:tokens, lane(t)]
        return carry

    lax.fori_loop(0, images, image_back, 0)
    for part in feed:
        part.gather_plane(depth - 1)
        part.stack()
    send_out.gather_plane(send_out.all)
    send_out.stack()

    def relative(tile, extent):
        bias_q = jnp.zeros((images, LANES), f32)
        bias_all = jnp.zeros((images, LANES), f32)
        dot_sum = jnp.zeros((images, LANES), f32)
        for n in range(tokens):
            grad = da_ref[tile, token(n), :]
            dq = (dq_ref[tile, token(n), :] + grad * conv_ref[tile, token(n), :]).astype(bf16)
            raw_ref[token(n), lane(tile)] = dq
            bias_q = bias_q + dq.astype(f32)
            dc = grad * q_ref[tile, token(n), :]
            dc_ref[tile, token(n), :] = dc
            if n > 0:
                bias_all = bias_all + dc
            dot_sum = dot_sum + dk_ref[tile, token(n), :] * ks_ref[tile, token(n), :]
        for n in range(tokens):
            soft = ks_ref[tile, token(n), :]
            raw_ref[token(n), lane(tile + 4)] = (soft * (dk_ref[tile, token(n), :] - dot_sum)).astype(bf16)
        sums_ref[OUT_BIAS_Q, :, lane(tile)] = fold_rows(bias_q)
        sums_ref[OUT_BIAS_ALL, :, lane(tile)] = fold_rows(bias_all)
        first = dv_ref[tile, token(0), :].astype(bf16)
        raw_ref[token(0), lane(tile + 8)] = first
        bias_v = [first.astype(f32)]

        def emit(i, total):
            for j in range(GRID):
                here = cell_rows(images, i * GRID + j)
                dv = (dv_ref[tile, here, :] + total[j]).astype(bf16)
                raw_ref[here, lane(tile + 8)] = dv
                bias_v[0] = bias_v[0] + dv.astype(f32)

        depthwise_rows(
            partial(grid_row, dc_ref, tile, images), lambda ab: prm(full_tap(extent, *ab), tile),
            extent, True, emit,
        )
        sums_ref[OUT_BIAS_V, :, lane(tile)] = fold_rows(bias_v[0])
        extra = (GRID - extent) // 2

        def emit_tap(a, b, total):
            sums_ref[OUT_KERNEL_ALL + (a + extra) * GRID + b + extra, :, lane(tile)] = fold_rows(total)

        kernel_grads(
            partial(grid_row, dc_ref, tile, images), partial(grid_row, v_ref, tile, images), extent, emit_tap
        )

    tile_extents(relative)
    for part in feed:
        part.settle()
    send_out.settle()

    for k in range(3):
        at = slice(k * width, (k + 1) * width)
        grad_joint = dot(h1_ref[...], raw_ref[:, at], 0, 0).astype(bf16)
        for t in range(depth):
            gj_ref[t, 0:share, at] = grad_joint[t * share : (t + 1) * share, :]
            if gj_ref.shape[1] > share:
                gj_ref[t, share:, at] = jnp.zeros((gj_ref.shape[1] - share, width), bf16)
    send_joint.pair(send_joint.all)
    dh1_ref = one_ref
    put_wide(dh1_ref, every, dot(raw_ref[...], wj_ref[...], 1, 1))
    send_joint.plane(send_joint.all)
    for part in feed:
        part.to_twin()
    send_out.to_twin()

    def back(k, carry):
        at = block_at(k)
        grad = wide(dh1_ref, at)
        unit, scale = normalise(wide(x1_ref, at))
        put_wide(da_ref, at, wide(x2_ref, at) + normalise_back(grad, gain_one, unit, scale))
        return carry[0] + fold_rows(grad * unit), carry[1] + fold_rows(grad)

    sums = lax.fori_loop(0, steps, back, (zero, zero))
    sums_ref[OUT_EARLY_GAIN] = sums[0]
    sums_ref[OUT_EARLY_SHIFT] = sums[1]

    def position_back(tile, carry):
        bias = [jnp.zeros((images, LANES), f32)]
        dx_ref[0:images, lane(tile)] = da_ref[tile, 0:images, :].astype(bf16)

        def emit(i, total):
            here = grid_row(da_ref, tile, images, i)
            for j in range(GRID):
                dx_ref[cell_rows(images, i * GRID + j), lane(tile)] = (here[j] + total[j]).astype(bf16)
                bias[0] = bias[0] + here[j]

        depthwise_rows(
            partial(grid_row, da_ref, tile, images),
            lambda ab: prm(ROW_POS_KERNEL + ab[0] * 3 + ab[1], tile),
            3, True, emit,
        )
        sums_ref[OUT_POS_BIAS, :, lane(tile)] = fold_rows(bias[0])

        def emit_tap(a, b, total):
            sums_ref[OUT_POS_KERNEL + a * 3 + b, :, lane(tile)] = fold_rows(total)

        kernel_grads(partial(grid_row, da_ref, tile, images), partial(x_row, tile), 3, emit_tap)
        return carry

    lax.fori_loop(0, 4, position_back, 0)
    send_joint.gather_plane(send_joint.all)
    send_joint.stack()

    small = jnp.sum(sums_ref[...], axis=1).astype(bf16)
    for t in range(depth):
        gs_ref[t] = jnp.zeros(gs_ref.shape[1:], bf16)
        gs_ref[t, 0 : small.shape[0], :] = small[:, t * share : (t + 1) * share]
    send_small.pair(send_small.all)
    send_small.plane(send_small.all)
    send_joint.settle()
    send_small.gather_plane(send_small.all)
    send_small.stack()
    send_joint.to_plane()
    send_small.settle()
    send_joint.to_twin()
    send_small.to_plane()
    send_small.to_twin()
    for part in (send_expand, send_reduce, send_out, send_joint, send_small):
        part.finish()
    for copy in ring.sent:
        copy.wait_send()


def pack_params(position_kernel, position_bias, early_gain, early_shift, joint_bias, small_kernel, small_bias,
                middle_kernel, middle_bias, large_kernel, large_bias, output_bias, late_gain, late_shift, reduce_bias):
    width = position_bias.shape[0]
    kernel_all = jnp.concatenate(
        [
            jnp.pad(small_kernel, ((2, 2), (2, 2), (0, 0))),
            jnp.pad(middle_kernel, ((1, 1), (1, 1), (0, 0))),
            large_kernel,
        ],
        axis=2,
    ).reshape(CELLS, width)
    return jnp.concatenate(
        [
            position_bias[None], early_gain[None], early_shift[None], joint_bias.reshape(2, width),
            jnp.concatenate([small_bias, middle_bias, large_bias])[None],
            output_bias[None], late_gain[None], late_shift[None], reduce_bias[None],
            position_kernel.reshape(9, width), kernel_all,
            jnp.zeros((PARAM_ROWS - ROW_KERNEL_ALL - CELLS, width), bf16),
        ],
        axis=0,
    ).astype(f32)


def per_device(
    block_input, position_kernel, position_bias, early_gain, early_shift, joint_weight, joint_bias,
    small_kernel, small_bias, middle_kernel, middle_bias, large_kernel, large_bias,
    output_weight, output_bias, late_gain, late_shift, expand_weight, expand_bias,
    reduce_weight, reduce_bias, cotangent,
):
    images, tokens, width = block_input.shape
    rows = images * tokens
    depth, copies_of = lax.axis_size("tensor"), lax.axis_size("dp")
    planes = math.gcd(copies_of // 2, 4)
    pieces = 2 * planes
    share, cw = width // depth, expand_weight.shape[1]
    params = pack_params(
        position_kernel, position_bias, early_gain, early_shift, joint_bias, small_kernel, small_bias,
        middle_kernel, middle_bias, large_kernel, large_bias, output_bias, late_gain, late_shift, reduce_bias,
    )
    unit = 16 * pieces
    sum_rows = padded(OUT_EXPAND_BIAS + depth, 16)
    shapes = [
        (padded(share, unit), width), (padded(width, unit), cw), (padded(cw, unit), width),
        (padded(share, unit), 3 * width), (padded(sum_rows, unit), share),
    ]
    near, far = planes - 1, depth - 1
    copies = 11 * far + (2 + far) * near + 2 + far + 2 * depth * (1 + near) + 3 * (1 + near) + 5 * near + 5
    fill = lambda array, count: jnp.pad(array, ((0, count - array.shape[0]), (0, 0)))
    tiled = pltpu.VMEM((4, rows, LANES), f32)
    low = pltpu.VMEM((rows, width), bf16)
    per_image = pltpu.VMEM((images, PAD_TOK, width), bf16)
    boxes = lambda lead: [pltpu.VMEM(lead + shape, bf16) for shape in shapes]
    halves = [pltpu.VMEM((depth, r // 2, w), bf16) for r, w in shapes]
    pieces_of = lambda lead: [pltpu.VMEM(lead + (r // pieces, w), bf16) for r, w in shapes]
    scratch = (
        [tiled] * 11
        + [low] * 3 + [pltpu.VMEM((rows, 3 * width), bf16)]
        + [per_image] * 4 + [pltpu.VMEM((images, HEAD, width), bf16)]
        + [pltpu.VMEM((sum_rows, 8, width), f32)]
        + [pltpu.VMEM((depth,) + shape, bf16) for shape in shapes[:3]] + [pltpu.VMEM((depth, 8, cw), f32)]
        + boxes((depth,)) + halves + pieces_of((planes - 1, depth)) + pieces_of((depth - 1,))
        + [pltpu.SemaphoreType.DMA((copies,))] * 2 + [pltpu.SemaphoreType.DMA((4,))]
    )
    flat = lambda array: array.transpose(1, 0, 2).reshape(rows, width)
    anywhere = pl.BlockSpec(memory_space=pl.ANY)
    inside = pl.BlockSpec(memory_space=pltpu.VMEM)
    outs = [
        ((rows, width), bf16), ((rows, width), bf16),
        (shapes[0], bf16), (shapes[1], bf16), (shapes[2], bf16),
        ((depth,) + shapes[3], bf16), ((depth,) + shapes[4], bf16),
    ]
    y, dx, gwo, gwe, gwr, gwj, small = pl.pallas_call(
        partial(whole_block, images, tokens, planes, depth),
        out_shape=[jax.ShapeDtypeStruct(shape, dtype) for shape, dtype in outs],
        in_specs=[inside] * 4 + [anywhere] * 4,
        out_specs=[inside] * len(outs),
        scratch_shapes=scratch,
        compiler_params=pltpu.CompilerParams(
            vmem_limit_bytes=VMEM_BYTES, collective_id=1, has_side_effects=True
        ),
    )(
        flat(block_input), flat(cotangent), params, joint_weight,
        fill(output_weight, shapes[0][0]), fill(expand_weight, shapes[1][0]), fill(reduce_weight, shapes[2][0]),
        jnp.broadcast_to(expand_bias.astype(f32)[None], (8, cw)),
    )
    if copies_of > pieces:
        groups = [list(range(first, copies_of, pieces)) for first in range(pieces)]
        gwo, gwe, gwr, gwj, small = lax.psum((gwo, gwe, gwr, gwj, small), "dp", axis_index_groups=groups)
    image_form = lambda array: array.reshape(tokens, images, width).transpose(1, 0, 2)
    small = small.astype(f32).transpose(1, 0, 2).reshape(-1, width)
    kernel_all = small[OUT_KERNEL_ALL : OUT_KERNEL_ALL + CELLS].reshape(GRID, GRID, width)
    bias_all = small[OUT_BIAS_ALL]
    one = small_kernel.shape[2]
    two = one + middle_kernel.shape[2]
    bias_row = lax.dynamic_slice_in_dim(small, OUT_EXPAND_BIAS + lax.axis_index("tensor"), 1, 0)
    return (
        image_form(y), image_form(dx), small[OUT_POS_KERNEL : OUT_POS_KERNEL + 9].reshape(3, 3, width),
        small[OUT_POS_BIAS], small[OUT_EARLY_GAIN], small[OUT_EARLY_SHIFT],
        gwj[:, :share].reshape(width, 3 * width).astype(f32),
        small[OUT_BIAS_Q : OUT_BIAS_V + 1].reshape(-1),
        kernel_all[2:5, 2:5, :one], bias_all[:one], kernel_all[1:6, 1:6, one:two], bias_all[one:two],
        kernel_all[:, :, two:], bias_all[two:],
        gwo[:share].astype(f32), small[OUT_OUT_BIAS], small[OUT_LATE_GAIN], small[OUT_LATE_SHIFT],
        gwe[:width].astype(f32), bias_row[0, :cw], gwr[:cw].astype(f32), small[OUT_REDUCE_BIAS],
    )


def solution(mesh):
    images = P(("dp", "tensor"), None, None)
    in_specs = (images,) + (P(),) * 12 + (
        P("tensor", None), P(), P(), P(), P(None, "tensor"), P("tensor"), P("tensor", None), P(), images,
    )
    out_specs = (images, images) + (P(),) * 12 + (
        P("tensor", None), P(), P(), P(), P(None, "tensor"), P("tensor"), P("tensor", None), P(),
    )
    return jax.shard_map(per_device, mesh=mesh, in_specs=in_specs, out_specs=out_specs, check_vma=False)
```

time: 479 us -> 175 us (0.37)
  waiting for transfers between devices: 227 us -> 0 us
  blocking collectives: 117 us -> 0 us
  Pallas kernels: 88 us -> 148 us
  between operations: 14.3 us -> 0.76 us
  local copies, waits for them, and re-layouts: 22.4 us -> 15.7 us
    reduce_scatter x3 -> x0, waiting for transfers between devices: 107 us -> none  [per_device(): lax.psum_scatter(part, 'tensor', scatter_dimension=0, tiled=True)]
    psum x2 -> x0, waiting for transfers between devices: 90.6 us -> none  [the longest x1 56.3 us: per_device(): lax.psum(lax.psum_scatter(part, 'tensor', scatter_dimension=0, tiled=True...]
    psum x1 -> x0, blocking collectives: 82.7 us -> none  [per_device(): lax.psum((gwj.astype(f32), small, late), ('dp', 'tensor'))]
    pallas_call x3 -> x1, Pallas kernels: 88 us -> 148 us  [per_device(): pl.pallas_call(partial(whole_block, images, tokens, planes, depth), out_s...]
    all_gather x2 -> x0, blocking collectives: 34.6 us -> none  [the longest x1 20.8 us: per_device(): whole_out = lax.all_gather(output_weight, 'tensor', axis=0, tiled=True)]
    all_gather x2 -> x0, waiting for transfers between devices: 26.6 us -> none  [the longest x1 26.6 us: per_device(): whole_reduce = lax.all_gather(reduce_weight, 'tensor')]
    unnamed x27 -> x12, local copies, waits for them, and re-layouts: 6.94 us -> 1.8 us
  transfers between devices with their start and end apart: 7 -> 0, of which waited for: 6 -> 0; matrix products, arithmetic and copies ran while one was open for 5% -> 0% of each run, Pallas kernels for 6% -> 0%
where the time goes in v3:
time: 175 us; the launch traced here: 174 us
  Pallas kernels  148 us (85%)
  local copies, waits for them, and re-layouts  15.7 us (9%)
  other arithmetic  9.68 us (6%)
    pallas_call x1, Pallas kernels, per_device(): pl.pallas_call(partial(whole_block, images, tokens, planes, depth), out_s...  148 us
    convert_element_type x1, other arithmetic, per_device(): gwj[:, :share].reshape(width, 3 * width).astype(f32)  3.51 us

profile of v3, /device:TPU:0, one launch (start us, length us, event | category | flops | bytes accessed | tf_op | source)
XLA Modules:
  0.0 174.1 jit_solution(15838587784036543812)
XLA Ops:
  0.7 0.7 broadcast_in_dim.33
  1.3 0.7 broadcast_in_dim.34
  2.0 0.7 broadcast_in_dim.35
  2.7 0.7 reshape.106
  3.4 0.8 pad_maximum_fusion
  4.2 0.7 broadcast_in_dim.37
  4.8 0.7 broadcast_in_dim.38
  5.5 0.7 broadcast_in_dim.39
  6.2 0.7 broadcast_in_dim.40
  6.9 0.7 reshape.107
  7.6 0.9 fusion.4
  8.5 0.4 concatenate.11
  9.0 0.7 convert_element_type.26.prm_ref
  9.6 1.3 broadcast_in_dim.42.eb_shard
  10.9 148.0 %shard_map.381 = (bf16[800,512]{1,0:T(8,128)(2,1)}, bf16[800,512]{1,0:T(8,128)(2,1)}, bf16[128,512]{1,0:T(8,128)(2,1)}, bf16[512,512]{1,0:T(8,128)(2,1)}, bf16[5...) custom-call(bf16[800,512]{1,0:T(8,128)(2,1)} %bitcast.32, ...), custom_call_target="tpu_custom_call" | custom-call | tf_op jit(solution)/shard_map/pallas_call | solution.py:802
  158.9 0.9 convert_bitcast_fusion
  159.8 0.6 reshape.111
  160.5 0.6 fusion.5
  161.1 0.0 copy-start.4
  161.1 3.5 %bitcast_convert_fusion = f32[512,1536]{1,0:T(8,128)} fusion(bf16[4,128,1536]{2,1,0:T(8,128)(2,1)} %get-tuple-element.32), kind=kLoop, calls=%fused_computation | loop fusion | flops 786432 | bytes 4718592 | tf_op jit(solution)/shard_map/convert_element_type | solution.py:829
  164.6 0.0 copy-start.3
  164.6 0.6 copy.49
  165.2 0.0 copy-start.2
  165.3 0.6 slice.90
  165.9 0.5 slice_bitcast_fusion
  166.4 0.6 slice.92
  167.0 0.6 fusion.6
  167.7 0.7 slice.94
  168.4 0.0 copy-done.4
  168.4 0.7 convert_element_type.30
  169.1 0.0 copy-done.3
  169.1 1.1 convert_element_type.31
  170.2 0.0 copy-start.1
  170.2 0.1 copy.51
  170.4 0.8 dynamic-slice_reduce_fusion
  171.2 0.0 copy-done.2
  171.2 0.0 copy-start
  171.2 1.1 convert_element_type.32
  172.3 0.0 copy-done.1
  172.3 0.9 copy.54
  173.2 0.0 copy-done
  173.2 0.9 copy.55
  (9 shorter events, 0.1 us)
Async XLA Ops:
  161.1 7.3 %copy-start.4 = (bf16[128,512]{1,0:T(8,128)(2,1)S(1)}, bf16[128,512]{1,0:T(8,128)(2,1)}, u32[]{:S(2)}) copy-start(bf16[128,512]{1,0:T(8,128)(2,1)} %get-tuple-element.33) | copy-start | bytes 393220
  164.6 4.5 %copy-start.3 = (bf16[512,512]{1,0:T(8,128)(2,1)S(1)}, bf16[512,512]{1,0:T(8,128)(2,1)}, u32[]{:S(2)}) copy-start(bf16[512,512]{1,0:T(8,128)(2,1)} %get-tuple-element.34) | copy-start | bytes 1572868
  165.2 5.9 %copy-start.2 = (bf16[512,512]{1,0:T(8,128)(2,1)S(1)}, bf16[512,512]{1,0:T(8,128)(2,1)}, u32[]{:S(2)}) copy-start(bf16[512,512]{1,0:T(8,128)(2,1)} %get-tuple-element.35) | copy-start | bytes 1572868
  170.2 2.1 %copy-start.1 = (bf16[800,512]{1,0:T(8,128)(2,1)S(1)}, bf16[800,512]{1,0:T(8,128)(2,1)}, u32[]{:S(2)}) copy-start(bf16[800,512]{1,0:T(8,128)(2,1)} %get-tuple-element.29) | copy-start | bytes 2457604
  171.2 2.0 %copy-start = (bf16[800,512]{1,0:T(8,128)(2,1)S(1)}, bf16[800,512]{1,0:T(8,128)(2,1)}, u32[]{:S(2)}) copy-start(bf16[800,512]{1,0:T(8,128)(2,1)} %get-tuple-element.30) | copy-start | bytes 2457604
